TPU v7x, 256 devices: a whole 4x4x8 slice. The times are simulated.
256 devices in a mesh: section: 4 (over z_lo), space: 64 (over y, x, z_hi, core).
Axes of the slice: x: 4, y: 4, z: 8 (z_hi: 2, z_lo: 4; z = z_hi * 4 + z_lo), core: 2. Of those that a mesh axis runs over, the one named last changes fastest.
Arguments:
- features: bfloat16 [1, 256, 128, 320], P(None, 'space'), may hold values from -30 to 30
- section_packs: bfloat16 [4, 11520, 640], P('section', None, 'space'), may hold values from -6 to 6
Outputs:
- output: bfloat16 [1, 256, 128, 320], P(None, 'space', 'section')
All inputs are finite; a program needn't handle non-finite values.
Results may differ from a plain program's by a relative error of at most 0.009.
Values may be sent and summed in bfloat16 or wider, within the bound.
A program may use at most 128 MiB of HBM per device.

v0:
```python
from functools import partial
import math

import jax
import jax.numpy as jnp
from jax import lax
from jax.sharding import Mesh
from jax.sharding import PartitionSpec as P

GROUPS = 32
SPACE = ("space_0", "space_1", "space_2", "space_3")


EPSILON = 1e-05


def for_sending(x):
    return jax.tree.map(lambda a: a.astype(jnp.bfloat16) if a.dtype == jnp.float32 else a, x)


def padded(x, sides, width):
    for axis, dim in sides:
        size, length = (lax.axis_size(axis), x.shape[dim])
        up = [(i, (i + 1) % size) for i in range(size - 1)]
        down = [(j, i) for i, j in up]
        last = lax.slice_in_dim(x, length - width, length, axis=dim)
        initial = lax.slice_in_dim(x, 0, width, axis=dim)
        before = lax.ppermute(last, axis, up)
        after = lax.ppermute(initial, axis, down)
        x = jnp.concatenate([before, x, after], axis=dim)
    return x


def over_axes(x, axes):
    for axis in axes:
        x = lax.psum(x, axis)
    return x


def passed_along(value, axis, steps):
    count = lax.axis_size(axis)
    initial, last = (max(0, -steps), min(count, count - steps))
    return lax.ppermute(value, axis, [(source, source + steps) for source in range(initial, last)])


def cut_along(x, dim, size):
    shape = x.shape
    tiles = x.reshape(*shape[:dim], size, shape[dim] // size, *shape[dim + 1 :])
    return jnp.moveaxis(tiles, dim, 0)


def sent_and_summed(x, axis, dim):
    tiles = cut_along(x, dim, lax.axis_size(axis))
    arrived = lax.all_to_all(tiles, axis, split_axis=0, concat_axis=0, tiled=True)
    return arrived.astype(jnp.float32).sum(axis=0)


def convolve_rows(field_ext, kernel, fan_in, stride):
    result = lax.conv_general_dilated(
        field_ext[None],
        kernel,
        (stride, stride),
        ((0, 0), (1, 1)),
        dimension_numbers=("NHWC", "HWIO", "NHWC"),
        preferred_element_type=jnp.float32,
    )[0]
    return result * (1.0 / math.sqrt(fan_in))


def kernel_at(flat_pack, offset, c_in, c_out):
    return flat_pack[offset : offset + 9 * c_in * c_out].reshape(3, 3, c_in, c_out)


def grouped_view(values):
    return values.reshape(-1, GROUPS, values.shape[-1] // GROUPS)


def normalize(values, group_mean, group_var):
    shape_in = values.shape
    grouped = values.reshape(shape_in[:-1] + (GROUPS, shape_in[-1] // GROUPS))
    normed = (grouped - group_mean[:, None]) / jnp.sqrt(group_var + EPSILON)[:, None]
    return normed.reshape(shape_in)


def activate_ext(raw_ext, group_mean, group_var, top_edge, bottom_edge, ghost_rows):
    activated = jax.nn.silu(normalize(raw_ext.astype(jnp.float32), group_mean, group_var))
    row_ids = lax.broadcasted_iota(jnp.int32, (raw_ext.shape[0], 1, 1), 0)
    dropped = (row_ids < ghost_rows) & top_edge | (
        row_ids >= raw_ext.shape[0] - ghost_rows
    ) & bottom_edge
    return jnp.where(dropped, 0.0, activated).astype(jnp.bfloat16)


def edge_rows(block, ghost_rows):
    return jnp.concatenate(
        [
            block[:ghost_rows].reshape(ghost_rows, -1),
            block[block.shape[0] - ghost_rows :].reshape(ghost_rows, -1),
        ],
        0,
    )


def add_rows(cycle_rows, block, ghost_rows):
    row_shape = (ghost_rows,) + block.shape[1:]
    return jnp.concatenate(
        [
            cycle_rows[:ghost_rows].reshape(row_shape),
            block,
            cycle_rows[3 * ghost_rows :].reshape(row_shape),
        ],
        0,
    )


def trim_rows(block, count):
    return block[count : block.shape[0] - count]


def branches(func):
    return [
        partial(func, 0),
        partial(func, 1),
        partial(func, 2),
        partial(func, 3),
        partial(func, 4),
    ]


def shards(features, section_packs):
    section_id = lax.axis_index("section")
    row_dev = lax.axis_index(SPACE)
    n_space = lax.axis_size(SPACE)
    top_edge = row_dev == 0
    bottom_edge = row_dev == n_space - 1
    micro_count, fine_rows, fine_cols, narrow = features.shape
    wide_ch = 2 * narrow
    square = narrow * narrow
    fine_shape = (fine_rows, fine_cols, narrow)
    coarse_shape = (fine_rows // 2, fine_cols // 2, wide_ch)
    fine_zero = jnp.zeros(fine_shape, jnp.bfloat16)
    coarse_zero = jnp.zeros(coarse_shape, jnp.bfloat16)
    is_fine = (section_id == 0) | (section_id == 3)
    gathered = lax.all_gather(section_packs, SPACE, axis=2, tiled=True)
    flat_pack = gathered.reshape(-1)
    ghost_rows = 2

    def row_rims(block_rims):
        return padded(for_sending(block_rims), ((SPACE, 0),), 2).astype(block_rims.dtype)

    spare = ghost_rows - 1
    fine_hidden_zero = jnp.zeros((fine_rows + 2 * spare, fine_cols, narrow), jnp.bfloat16)
    coarse_hidden_zero = jnp.zeros(
        (fine_rows // 2 + 2 * spare, fine_cols // 2, wide_ch), jnp.bfloat16
    )

    def moments(branch_pick, source):
        empty = jnp.zeros((GROUPS,), jnp.float32)

        def pair_sums(branch_id):
            if branch_id == 4:
                return (empty, empty)
            grouped = grouped_view(source(branch_id))
            factor = 1.0 / (grouped.shape[0] * grouped.shape[2] * n_space)
            return (
                jnp.sum(grouped, axis=(0, 2)) * factor,
                jnp.sum(jnp.square(grouped), axis=(0, 2)) * factor,
            )

        first_part, second_part = lax.switch(branch_pick, branches(pair_sums))
        group_mean, mean_square = (over_axes(first_part, SPACE), over_axes(second_part, SPACE))
        return (group_mean, mean_square - group_mean * group_mean)

    def section_tick(tick_id, loop_state):
        handoff, skip_store, results = loop_state
        micro_id = tick_id - section_id
        active = (micro_id >= 0) & (micro_id < micro_count)
        micro_slot = jnp.clip(micro_id, 0, micro_count - 1)
        branch_pick = jnp.where(active, section_id, 4)
        kept_skip = lax.dynamic_index_in_dim(
            skip_store, jnp.clip(tick_id - 3, 0, micro_count - 1), 0, keepdims=False
        )
        skip_ext = passed_along(kept_skip, "section", 3)
        skip_inner = trim_rows(skip_ext, ghost_rows)
        cycle_in = row_rims(edge_rows(handoff, ghost_rows))

        def section_entry(branch_id):
            if branch_id == 0:
                return (
                    lax.dynamic_index_in_dim(features, micro_slot, 0, keepdims=False),
                    coarse_zero,
                )
            if branch_id == 3:
                coarse_ext = trim_rows(add_rows(cycle_in, handoff, ghost_rows), spare)
                upsampled = jnp.repeat(jnp.repeat(coarse_ext, 2, 0), 2, 1)[1:-1]
                made = convolve_rows(
                    upsampled, kernel_at(flat_pack, 0, wide_ch, narrow), 9 * wide_ch, 1
                )
                return (made.astype(jnp.bfloat16), coarse_zero)
            if branch_id == 4:
                return (fine_zero, coarse_zero)
            return (fine_zero, handoff)

        fine_in, coarse_in = lax.switch(branch_pick, branches(section_entry))

        def block_input(branch_id):
            if branch_id == 0:
                return fine_in.astype(jnp.float32)
            if branch_id == 3:
                return jnp.concatenate([fine_in, skip_inner], -1).astype(jnp.float32)
            return coarse_in.astype(jnp.float32)

        mean_one, var_one = moments(branch_pick, block_input)
        cycle_one = row_rims(
            jnp.where(is_fine, edge_rows(fine_in, ghost_rows), edge_rows(coarse_in, ghost_rows))
        )

        def first_conv(branch_id):
            if branch_id == 4:
                return (fine_hidden_zero, coarse_hidden_zero)
            if branch_id in (1, 2):
                activated = activate_ext(
                    add_rows(cycle_one, coarse_in, ghost_rows),
                    mean_one,
                    var_one,
                    top_edge,
                    bottom_edge,
                    ghost_rows,
                )
                made = convolve_rows(
                    activated, kernel_at(flat_pack, 0, wide_ch, wide_ch), 9 * wide_ch, 1
                )
                return (fine_hidden_zero, made.astype(jnp.bfloat16))
            raw_ext = add_rows(cycle_one, fine_in, ghost_rows)
            c_in = narrow
            offset = 0
            if branch_id == 3:
                raw_ext = jnp.concatenate([raw_ext, skip_ext], -1)
                c_in = wide_ch
                offset = 18 * square
            activated = activate_ext(raw_ext, mean_one, var_one, top_edge, bottom_edge, ghost_rows)
            made = convolve_rows(activated, kernel_at(flat_pack, offset, c_in, narrow), 9 * c_in, 1)
            return (made.astype(jnp.bfloat16), coarse_hidden_zero)

        hidden_fine, hidden_coarse = lax.switch(branch_pick, branches(first_conv))

        def hidden_input(branch_id):
            if branch_id in (0, 3):
                return trim_rows(hidden_fine, spare).astype(jnp.float32)
            return trim_rows(hidden_coarse, spare).astype(jnp.float32)

        mean_two, var_two = moments(branch_pick, hidden_input)

        def second_conv(branch_id):
            if branch_id == 4:
                return (fine_zero, coarse_zero)
            if branch_id in (1, 2):
                activated = activate_ext(hidden_coarse, mean_two, var_two, top_edge, bottom_edge, 1)
                update = convolve_rows(
                    activated, kernel_at(flat_pack, 36 * square, wide_ch, wide_ch), 9 * wide_ch, 1
                )
                return (fine_zero, (coarse_in.astype(jnp.float32) + update).astype(jnp.bfloat16))
            activated = activate_ext(hidden_fine, mean_two, var_two, top_edge, bottom_edge, 1)
            if branch_id == 0:
                update = convolve_rows(
                    activated, kernel_at(flat_pack, 9 * square, narrow, narrow), 9 * narrow, 1
                )
                return ((fine_in.astype(jnp.float32) + update).astype(jnp.bfloat16), coarse_zero)
            update = convolve_rows(
                activated, kernel_at(flat_pack, 36 * square, narrow, narrow), 9 * narrow, 1
            )
            joined = jnp.concatenate([fine_in, skip_inner], -1)
            projection = jnp.dot(
                joined.reshape(-1, wide_ch),
                flat_pack[45 * square : 47 * square].reshape(wide_ch, narrow),
                preferred_element_type=jnp.float32,
            )
            projection = projection.reshape(fine_shape) * (1.0 / math.sqrt(wide_ch))
            return ((projection + update).astype(jnp.bfloat16), coarse_zero)

        out_fine, out_coarse = lax.switch(branch_pick, branches(second_conv))
        cycle_three = row_rims(edge_rows(out_fine, ghost_rows))
        made_skip = add_rows(cycle_three, out_fine, ghost_rows)

        def section_exit(branch_id):
            if branch_id == 0:
                made = convolve_rows(
                    trim_rows(made_skip, spare),
                    kernel_at(flat_pack, 18 * square, narrow, wide_ch),
                    9 * narrow,
                    2,
                )
                return made.astype(jnp.bfloat16)
            if branch_id in (1, 2):
                return out_coarse
            return coarse_zero

        coarse_out = lax.switch(branch_pick, branches(section_exit))
        next_handoff = jax.tree.map(
            lambda part, own: part.astype(own.dtype),
            passed_along(for_sending(coarse_out), "section", 1),
            coarse_out,
        )
        store_here = (section_id == 0) & active
        current = lax.dynamic_index_in_dim(skip_store, micro_slot, 0, keepdims=False)
        skip_store = lax.dynamic_update_index_in_dim(
            skip_store, jnp.where(store_here, made_skip, current), micro_slot, 0
        )
        result_now = lax.dynamic_index_in_dim(results, micro_slot, 0, keepdims=False)
        results = lax.dynamic_update_index_in_dim(
            results, jnp.where((section_id == 3) & active, out_fine, result_now), micro_slot, 0
        )
        return (next_handoff, skip_store, results)

    skip_start = jnp.zeros(
        (micro_count, fine_rows + 2 * ghost_rows, fine_cols, narrow), jnp.bfloat16
    )
    result_start = jnp.zeros((micro_count,) + fine_shape, jnp.bfloat16)
    final_state = lax.fori_loop(
        0, micro_count + 3, section_tick, (coarse_zero, skip_start, result_start)
    )
    results = final_state[2]
    return sent_and_summed(results.astype(jnp.float32).astype(jnp.bfloat16), "section", 2).astype(
        jnp.bfloat16
    )


def solution(mesh):
    finer = Mesh(
        mesh.devices.reshape(mesh.shape["section"], 4, 4, 2, 2),
        ("section", "space_0", "space_1", "space_2", "space_3"),
    )
    in_specs = (P(None, SPACE, None, None), P("section", None, SPACE))
    out_specs = P(None, SPACE, "section", None)
    return jax.shard_map(
        shards, mesh=finer, in_specs=in_specs, out_specs=out_specs, check_vma=False
    )
```

profile of v0, /device:TPU:64, one launch (start us, length us, event | category | flops | bytes accessed | tf_op | source)
XLA Modules:
  0.0 1101.2 jit_solution(12961522220352120533)
XLA Ops:
  8.7 226.2 %all-gather.2.cloned.1.call-done = bf16[1,11520,640]{1,0,2:T(2,128)(2,1)} async-done(((bf16[1,11520,10]{1,0,2:T(2,128)(2,1)}), bf16[1,11520,640]{1,0,2:T(2,128)(2,1)}) %all-gather.2.cloned.1.call-update) | async-done | bytes 14745616 | tf_op jit(solution)/shard_map/all_gather | solution.py:144
  235.0 56.7 %copy.149 = bf16[1,11520,640]{2,1,0:T(8,128)(2,1)} copy(bf16[1,11520,640]{1,0,2:T(2,128)(2,1)} %all-gather.2.cloned.1.call-done) | data formatting | bytes 29491200 | tf_op jit(solution)/shard_map/all_gather | solution.py:144
  291.7 24.5 %reshape.731 = bf16[7372800]{0:T(1024)(128)(2,1)} reshape(bf16[1,11520,640]{2,1,0:T(8,128)(2,1)} %copy.149) | data formatting | bytes 29491200 | tf_op jit(solution)/shard_map/reshape | solution.py:145
  317.0 763.2 %while.25 = (s32[]{:T(128)}, bf16[2,64,640]{2,0,1:T(2,128)(2,1)S(1)}, bf16[1,8,128,320]{2,3,1,0:T(8,128)(2,1)}, bf16[1,4,128,320]{2,3,1,0:T(8,128)(2,1)}, s32[]{...) while((s32[]{:T(128)}, ...), condition=%wide.region_79.80_spmd.clone, body=%wide.region_0.79_spmd.clone.sunk | while | flops 6792821760 | bytes 173504272 | solution.py:319
  327.1 30.6 %collective-permute-start.2 = (bf16[2,40960]{1,0:T(2,128)(2,1)S(1)}, bf16[2,40960]{1,0:T(2,128)(2,1)S(1)}, u32[]{:S(2)}, u32[]{:S(2)}) collective-permute-start(bf16[2,40960]{1,0:T(2,128)(2,1)S(1)} %get-tuple-element.923), channel_id=1, source_target_pairs={{0,1},{1,2},{2,3},{3,4},{4,5},{5,6},{6,7},{7,8},{8,9},{9,10},{10,1... | collective-permute-start | bytes 491528 | tf_op jit(solution)/shard_map/while/body/eval_jaxpr/ppermute | solution.py:28
  360.1 12.7 %all-reduce.16 = (f32[32]{0:T(128)S(1)}, f32[32]{0:T(128)S(1)}) all-reduce(f32[32]{0:T(128)S(1)} %get-tuple-element.925, f32[32]{0:T(128)S(1)} %get-tuple-element.926), channel_id=1, replica_groups=mesh['section'=4,'space_0'=4,'space_1'=4,'space_2'=2,'space_3'=2] {'spac..., use_global_device_ids=true, to_apply=%region_27.27 | all-reduce | flops 64 | bytes 512 | tf_op jit(solution)/shard_map/while/body/eval_jaxpr/psum | solution.py:36
  372.8 7.7 all-reduce.17
  380.5 8.8 all-reduce.18
  391.8 19.6 %conditional.20 = (bf16[6,128,320]{2,1,0:T(8,128)(2,1)S(1)}, bf16[4,64,640]{2,1,0:T(8,128)(2,1)S(1)}) conditional(s32[]{:T(128)} %clamp.15, (pred[]{:T(512)}, pred[]{:T(512)}, bf16[2,40960]{1,0:T(2,128)(2,1)S(1)}, bf16[4,128,320]{2,0,1:T(4,128)(2,1)S(1)}, bf16[2,40960]{1,0:T(2,128)(2,1)S(1)}, ...), branch_computations={%region_35.35_spmd.clone, %region_36.36_spmd.clone, %region_37.37_... | conditional | flops 3024696320 | bytes 44130212 | solution.py:245
  411.5 7.7 all-reduce.20
  419.2 9.7 all-reduce.21
  428.9 8.8 all-reduce.22
  460.5 8.7 collective-permute-start
  473.2 8.1 collective-permute-done.1
  483.3 9.8 collective-permute-start.2
  495.5 19.7 %all-reduce.16 = (f32[32]{0:T(128)S(1)}, f32[32]{0:T(128)S(1)}) all-reduce(f32[32]{0:T(128)S(1)} %get-tuple-element.925, f32[32]{0:T(128)S(1)} %get-tuple-element.926), channel_id=1, replica_groups=mesh['section'=4,'space_0'=4,'space_1'=4,'space_2'=2,'space_3'=2] {'spac..., use_global_device_ids=true, to_apply=%region_27.27 | all-reduce | flops 64 | bytes 512 | tf_op jit(solution)/shard_map/while/body/eval_jaxpr/psum | solution.py:36
  515.1 7.7 all-reduce.17
  522.9 8.8 all-reduce.18
  534.2 19.3 %conditional.20 = (bf16[6,128,320]{2,1,0:T(8,128)(2,1)S(1)}, bf16[4,64,640]{2,1,0:T(8,128)(2,1)S(1)}) conditional(s32[]{:T(128)} %clamp.15, (pred[]{:T(512)}, pred[]{:T(512)}, bf16[2,40960]{1,0:T(2,128)(2,1)S(1)}, bf16[4,128,320]{2,0,1:T(4,128)(2,1)S(1)}, bf16[2,40960]{1,0:T(2,128)(2,1)S(1)}, ...), branch_computations={%region_35.35_spmd.clone, %region_36.36_spmd.clone, %region_37.37_... | conditional | flops 3024696320 | bytes 44130212 | solution.py:245
  553.5 7.8 all-reduce.20
  561.3 9.9 all-reduce.21
  571.2 8.8 all-reduce.22
  595.2 25.6 %collective-permute-start.7 = (bf16[2,64,640]{2,0,1:T(2,128)(2,1)S(1)}, bf16[2,64,640]{2,0,1:T(2,128)(2,1)S(1)}, u32[]{:S(2)}, u32[]{:S(2)}) collective-permute-start(bf16[2,64,640]{2,0,1:T(2,128)(2,1)S(1)} %get-tuple-element.1046), channel_id=1, source_target_pairs={{0,64},{64,128},{128,192},{1,65},{65,129},{129,193},{2,66},{66,130... | collective-permute-start | bytes 491528 | tf_op jit(solution)/shard_map/while/body/eval_jaxpr/ppermute | solution.py:43
  622.9 56.2 %collective-permute-done.7 = bf16[2,64,640]{2,0,1:T(2,128)(2,1)S(1)} collective-permute-done((bf16[2,64,640]{2,0,1:T(2,128)(2,1)S(1)}, bf16[2,64,640]{2,0,1:T(2,128)(2,1)S(1)}, u32[]{:S(2)}, u32[]{:S(2)}) %collective-permute-start.7) | collective-permute-done | bytes 163872 | tf_op jit(solution)/shard_map/while/body/eval_jaxpr/ppermute | solution.py:43
  679.2 7.6 collective-permute-start
  698.9 28.2 %collective-permute-start.2 = (bf16[2,40960]{1,0:T(2,128)(2,1)S(1)}, bf16[2,40960]{1,0:T(2,128)(2,1)S(1)}, u32[]{:S(2)}, u32[]{:S(2)}) collective-permute-start(bf16[2,40960]{1,0:T(2,128)(2,1)S(1)} %get-tuple-element.923), channel_id=1, source_target_pairs={{0,1},{1,2},{2,3},{3,4},{4,5},{5,6},{6,7},{7,8},{8,9},{9,10},{10,1... | collective-permute-start | bytes 491528 | tf_op jit(solution)/shard_map/while/body/eval_jaxpr/ppermute | solution.py:28
  730.0 14.4 %all-reduce.16 = (f32[32]{0:T(128)S(1)}, f32[32]{0:T(128)S(1)}) all-reduce(f32[32]{0:T(128)S(1)} %get-tuple-element.925, f32[32]{0:T(128)S(1)} %get-tuple-element.926), channel_id=1, replica_groups=mesh['section'=4,'space_0'=4,'space_1'=4,'space_2'=2,'space_3'=2] {'spac..., use_global_device_ids=true, to_apply=%region_27.27 | all-reduce | flops 64 | bytes 512 | tf_op jit(solution)/shard_map/while/body/eval_jaxpr/psum | solution.py:36
  744.4 7.7 all-reduce.17
  752.1 8.8 all-reduce.18
  763.4 39.4 %conditional.20 = (bf16[6,128,320]{2,1,0:T(8,128)(2,1)S(1)}, bf16[4,64,640]{2,1,0:T(8,128)(2,1)S(1)}) conditional(s32[]{:T(128)} %clamp.15, (pred[]{:T(512)}, pred[]{:T(512)}, bf16[2,40960]{1,0:T(2,128)(2,1)S(1)}, bf16[4,128,320]{2,0,1:T(4,128)(2,1)S(1)}, bf16[2,40960]{1,0:T(2,128)(2,1)S(1)}, ...), branch_computations={%region_35.35_spmd.clone, %region_36.36_spmd.clone, %region_37.37_... | conditional | flops 3024696320 | bytes 44130212 | solution.py:245
  769.7 6.5 slice.219
  776.3 12.8 %slice.220 = bf16[3,3,640,640]{3,2,1,0:T(8,128)(2,1)} reshape(bf16[3686400]{0:T(1024)(128)(2,1)} %slice.219) | data formatting | bytes 14745600 | tf_op jit(solution)/shard_map/while/body/eval_jaxpr/cond/branch_2_fun/slice | solution.py:71
  803.4 7.7 all-reduce.20
  811.1 9.7 all-reduce.21
  820.8 8.8 all-reduce.22
  832.1 26.2 %conditional.22 = (bf16[4,128,320]{1,2,0:T(8,128)(2,1)S(1)}, bf16[2,64,640]{2,1,0:T(8,128)(2,1)S(1)}) conditional(s32[]{:T(128)} %clamp.15, (bf16[4,128,320]{2,0,1:T(4,128)(2,1)S(1)}, pred[]{:T(512)}, pred[]{:T(512)}, bf16[6,128,320]{2,1,0:T(8,128)(2,1)S(1)}, f32[32]{0:T(128)S(1)}, /*index=5*/f32[32]{0:T(128)S(1)}, ...), branch_computations={%region_69.69_spmd, %region_70.70_spmd, %region_71.71_spmd, %regio... | conditional | flops 1218529280 | bytes 41974688 | solution.py:281
  840.0 12.8 %slice.202 = bf16[3,3,640,640]{3,2,1,0:T(8,128)(2,1)} reshape(bf16[3686400]{0:T(1024)(128)(2,1)} %slice.201) | data formatting | bytes 14745600 | tf_op jit(solution)/shard_map/while/body/eval_jaxpr/cond/branch_2_fun/slice | solution.py:71
  875.3 7.0 collective-permute-start
  894.7 28.2 %collective-permute-start.2 = (bf16[2,40960]{1,0:T(2,128)(2,1)S(1)}, bf16[2,40960]{1,0:T(2,128)(2,1)S(1)}, u32[]{:S(2)}, u32[]{:S(2)}) collective-permute-start(bf16[2,40960]{1,0:T(2,128)(2,1)S(1)} %get-tuple-element.923), channel_id=1, source_target_pairs={{0,1},{1,2},{2,3},{3,4},{4,5},{5,6},{6,7},{7,8},{8,9},{9,10},{10,1... | collective-permute-start | bytes 491528 | tf_op jit(solution)/shard_map/while/body/eval_jaxpr/ppermute | solution.py:28
  925.3 14.4 %all-reduce.16 = (f32[32]{0:T(128)S(1)}, f32[32]{0:T(128)S(1)}) all-reduce(f32[32]{0:T(128)S(1)} %get-tuple-element.925, f32[32]{0:T(128)S(1)} %get-tuple-element.926), channel_id=1, replica_groups=mesh['section'=4,'space_0'=4,'space_1'=4,'space_2'=2,'space_3'=2] {'spac..., use_global_device_ids=true, to_apply=%region_27.27 | all-reduce | flops 64 | bytes 512 | tf_op jit(solution)/shard_map/while/body/eval_jaxpr/psum | solution.py:36
  939.6 7.7 all-reduce.17
  947.4 8.8 all-reduce.18
  958.7 19.3 %conditional.20 = (bf16[6,128,320]{2,1,0:T(8,128)(2,1)S(1)}, bf16[4,64,640]{2,1,0:T(8,128)(2,1)S(1)}) conditional(s32[]{:T(128)} %clamp.15, (pred[]{:T(512)}, pred[]{:T(512)}, bf16[2,40960]{1,0:T(2,128)(2,1)S(1)}, bf16[4,128,320]{2,0,1:T(4,128)(2,1)S(1)}, bf16[2,40960]{1,0:T(2,128)(2,1)S(1)}, ...), branch_computations={%region_35.35_spmd.clone, %region_36.36_spmd.clone, %region_37.37_... | conditional | flops 3024696320 | bytes 44130212 | solution.py:245
  978.0 7.7 all-reduce.20
  985.8 9.7 all-reduce.21
  995.5 8.8 all-reduce.22
  1019.5 56.6 %collective-permute-start.7 = (bf16[2,64,640]{2,0,1:T(2,128)(2,1)S(1)}, bf16[2,64,640]{2,0,1:T(2,128)(2,1)S(1)}, u32[]{:S(2)}, u32[]{:S(2)}) collective-permute-start(bf16[2,64,640]{2,0,1:T(2,128)(2,1)S(1)} %get-tuple-element.1046), channel_id=1, source_target_pairs={{0,64},{64,128},{128,192},{1,65},{65,129},{129,193},{2,66},{66,130... | collective-permute-start | bytes 491528 | tf_op jit(solution)/shard_map/while/body/eval_jaxpr/ppermute | solution.py:43
  1081.5 11.9 %all_to_all.5 = bf16[4,1,4,32,320]{4,3,2,1,0:T(8,128)(2,1)S(1)} all-to-all(bf16[4,1,4,32,320]{4,3,2,1,0:T(8,128)(2,1)S(1)} %copy.151), channel_id=1, replica_groups=mesh['section'=4,'space_0'=4,'space_1'=4,'space_2'=2,'space_3'=2] {'sect..., dimensions={0} | all-to-all | bytes 655360 | tf_op jit(solution)/shard_map/all_to_all | solution.py:54
  (307 shorter events, 164.7 us)
Async XLA Ops:
  6.5 228.4 %all-gather.2.cloned.1.call-start = ((), (), s32[]{:S(2)}) async-start(), calls=%async_computation.1 | async-start | bytes 29952000 | tf_op jit(solution)/shard_map/all_gather | solution.py:144
  291.7 25.3 %copy-start.3 = (bf16[1,4,128,320]{2,3,1,0:T(8,128)(2,1)S(1)}, bf16[1,4,128,320]{2,3,1,0:T(8,128)(2,1)}, u32[]{:S(2)}) copy-start(bf16[1,4,128,320]{2,3,1,0:T(8,128)(2,1)} %param.34) | copy-start | bytes 983044
  317.3 5.1 collective-permute-start
  319.4 5.6 collective-permute-start.1
  320.8 38.2 %collective-permute-start.4 = (bf16[8,128,320]{1,2,0:T(8,128)(2,1)S(1)}, bf16[8,128,320]{1,2,0:T(8,128)(2,1)}, u32[]{:S(2)}, u32[]{:S(2)}) collective-permute-start(bf16[8,128,320]{1,2,0:T(8,128)(2,1)S(1)} %fusion.186), channel_id=1, source_target_pairs={{0,192},{1,193},{2,194},{3,195},{4,196},{5,197},{6,198},{7,199},{8... | collective-permute-start | bytes 1966088 | tf_op jit(solution)/shard_map/while/body/eval_jaxpr/ppermute | solution.py:43
  327.1 64.7 %collective-permute-start.2 = (bf16[2,40960]{1,0:T(2,128)(2,1)S(1)}, bf16[2,40960]{1,0:T(2,128)(2,1)S(1)}, u32[]{:S(2)}, u32[]{:S(2)}) collective-permute-start(bf16[2,40960]{1,0:T(2,128)(2,1)S(1)} %get-tuple-element.923), channel_id=1, source_target_pairs={{0,1},{1,2},{2,3},{3,4},{4,5},{5,6},{6,7},{7,8},{8,9},{9,10},{10,1... | collective-permute-start | bytes 491528 | tf_op jit(solution)/shard_map/while/body/eval_jaxpr/ppermute | solution.py:28
  357.7 34.1 %collective-permute-start.3 = (bf16[2,40960]{1,0:T(2,128)(2,1)S(1)}, bf16[2,40960]{1,0:T(2,128)(2,1)S(1)}, u32[]{:S(2)}, u32[]{:S(2)}) collective-permute-start(bf16[2,40960]{1,0:T(2,128)(2,1)S(1)} %get-tuple-element.924), channel_id=1, source_target_pairs={{1,0},{2,1},{3,2},{4,3},{5,4},{6,5},{7,6},{8,7},{9,8},{10,9},{11,1... | collective-permute-start | bytes 491528 | tf_op jit(solution)/shard_map/while/body/eval_jaxpr/ppermute | solution.py:29
  445.3 5.5 copy-start.1
  446.0 4.9 collective-permute-start.5
  447.7 4.0 collective-permute-start.6
  450.9 1.9 copy-start.2
  453.0 7.4 copy-start.4
  453.0 7.3 collective-permute-start.7
  460.5 12.7 %collective-permute-start = (bf16[2,40960]{1,0:T(2,128)(2,1)S(1)}, bf16[2,40960]{1,0:T(2,128)(2,1)S(1)}, u32[]{:S(2)}, u32[]{:S(2)}) collective-permute-start(bf16[2,40960]{1,0:T(2,128)(2,1)S(1)} %bitcast.199), channel_id=1, source_target_pairs={{0,1},{1,2},{2,3},{3,4},{4,5},{5,6},{6,7},{7,8},{8,9},{9,10},{10,1... | collective-permute-start | bytes 491528 | tf_op jit(solution)/shard_map/while/body/eval_jaxpr/ppermute | solution.py:28
  469.2 12.1 %collective-permute-start.1 = (bf16[2,40960]{1,0:T(2,128)(2,1)S(1)}, bf16[2,40960]{1,0:T(2,128)(2,1)S(1)}, u32[]{:S(2)}, u32[]{:S(2)}) collective-permute-start(bf16[2,40960]{1,0:T(2,128)(2,1)S(1)} %bitcast.200), channel_id=1, source_target_pairs={{1,0},{2,1},{3,2},{4,3},{5,4},{6,5},{7,6},{8,7},{9,8},{10,9},{11,1... | collective-permute-start | bytes 491528 | tf_op jit(solution)/shard_map/while/body/eval_jaxpr/ppermute | solution.py:29
  471.6 22.8 %collective-permute-start.4 = (bf16[8,128,320]{1,2,0:T(8,128)(2,1)S(1)}, bf16[8,128,320]{1,2,0:T(8,128)(2,1)}, u32[]{:S(2)}, u32[]{:S(2)}) collective-permute-start(bf16[8,128,320]{1,2,0:T(8,128)(2,1)S(1)} %fusion.186), channel_id=1, source_target_pairs={{0,192},{1,193},{2,194},{3,195},{4,196},{5,197},{6,198},{7,199},{8... | collective-permute-start | bytes 1966088 | tf_op jit(solution)/shard_map/while/body/eval_jaxpr/ppermute | solution.py:43
  483.3 50.9 %collective-permute-start.2 = (bf16[2,40960]{1,0:T(2,128)(2,1)S(1)}, bf16[2,40960]{1,0:T(2,128)(2,1)S(1)}, u32[]{:S(2)}, u32[]{:S(2)}) collective-permute-start(bf16[2,40960]{1,0:T(2,128)(2,1)S(1)} %get-tuple-element.923), channel_id=1, source_target_pairs={{0,1},{1,2},{2,3},{3,4},{4,5},{5,6},{6,7},{7,8},{8,9},{9,10},{10,1... | collective-permute-start | bytes 491528 | tf_op jit(solution)/shard_map/while/body/eval_jaxpr/ppermute | solution.py:28
  493.1 41.1 %collective-permute-start.3 = (bf16[2,40960]{1,0:T(2,128)(2,1)S(1)}, bf16[2,40960]{1,0:T(2,128)(2,1)S(1)}, u32[]{:S(2)}, u32[]{:S(2)}) collective-permute-start(bf16[2,40960]{1,0:T(2,128)(2,1)S(1)} %get-tuple-element.924), channel_id=1, source_target_pairs={{1,0},{2,1},{3,2},{4,3},{5,4},{6,5},{7,6},{8,7},{9,8},{10,9},{11,1... | collective-permute-start | bytes 491528 | tf_op jit(solution)/shard_map/while/body/eval_jaxpr/ppermute | solution.py:29
  587.6 5.5 copy-start.1
  588.3 4.9 collective-permute-start.5
  590.0 4.0 collective-permute-start.6
  593.1 1.9 copy-start.2
  595.2 83.9 %copy-start.4 = (bf16[1,4,128,320]{2,3,1,0:T(8,128)(2,1)S(1)}, bf16[1,4,128,320]{2,3,1,0:T(8,128)(2,1)}, u32[]{:S(2)}) copy-start(bf16[1,4,128,320]{2,3,1,0:T(8,128)(2,1)} %get-tuple-element.1072) | copy-start | bytes 983044 | tf_op jit(solution)/shard_map/while
  595.2 83.9 %collective-permute-start.7 = (bf16[2,64,640]{2,0,1:T(2,128)(2,1)S(1)}, bf16[2,64,640]{2,0,1:T(2,128)(2,1)S(1)}, u32[]{:S(2)}, u32[]{:S(2)}) collective-permute-start(bf16[2,64,640]{2,0,1:T(2,128)(2,1)S(1)} %get-tuple-element.1046), channel_id=1, source_target_pairs={{0,64},{64,128},{128,192},{1,65},{65,129},{129,193},{2,66},{66,130... | collective-permute-start | bytes 491528 | tf_op jit(solution)/shard_map/while/body/eval_jaxpr/ppermute | solution.py:43
  679.2 11.6 %collective-permute-start = (bf16[2,40960]{1,0:T(2,128)(2,1)S(1)}, bf16[2,40960]{1,0:T(2,128)(2,1)S(1)}, u32[]{:S(2)}, u32[]{:S(2)}) collective-permute-start(bf16[2,40960]{1,0:T(2,128)(2,1)S(1)} %bitcast.199), channel_id=1, source_target_pairs={{0,1},{1,2},{2,3},{3,4},{4,5},{5,6},{6,7},{7,8},{8,9},{9,10},{10,1... | collective-permute-start | bytes 491528 | tf_op jit(solution)/shard_map/while/body/eval_jaxpr/ppermute | solution.py:28
  686.8 10.0 collective-permute-start.1
  689.3 39.2 %collective-permute-start.4 = (bf16[8,128,320]{1,2,0:T(8,128)(2,1)S(1)}, bf16[8,128,320]{1,2,0:T(8,128)(2,1)}, u32[]{:S(2)}, u32[]{:S(2)}) collective-permute-start(bf16[8,128,320]{1,2,0:T(8,128)(2,1)S(1)} %fusion.186), channel_id=1, source_target_pairs={{0,192},{1,193},{2,194},{3,195},{4,196},{5,197},{6,198},{7,199},{8... | collective-permute-start | bytes 1966088 | tf_op jit(solution)/shard_map/while/body/eval_jaxpr/ppermute | solution.py:43
  698.9 64.5 %collective-permute-start.2 = (bf16[2,40960]{1,0:T(2,128)(2,1)S(1)}, bf16[2,40960]{1,0:T(2,128)(2,1)S(1)}, u32[]{:S(2)}, u32[]{:S(2)}) collective-permute-start(bf16[2,40960]{1,0:T(2,128)(2,1)S(1)} %get-tuple-element.923), channel_id=1, source_target_pairs={{0,1},{1,2},{2,3},{3,4},{4,5},{5,6},{6,7},{7,8},{8,9},{9,10},{10,1... | collective-permute-start | bytes 491528 | tf_op jit(solution)/shard_map/while/body/eval_jaxpr/ppermute | solution.py:28
  727.2 36.2 %collective-permute-start.3 = (bf16[2,40960]{1,0:T(2,128)(2,1)S(1)}, bf16[2,40960]{1,0:T(2,128)(2,1)S(1)}, u32[]{:S(2)}, u32[]{:S(2)}) collective-permute-start(bf16[2,40960]{1,0:T(2,128)(2,1)S(1)} %get-tuple-element.924), channel_id=1, source_target_pairs={{1,0},{2,1},{3,2},{4,3},{5,4},{6,5},{7,6},{8,7},{9,8},{10,9},{11,1... | collective-permute-start | bytes 491528 | tf_op jit(solution)/shard_map/while/body/eval_jaxpr/ppermute | solution.py:29
  776.2 12.8 %copy-start.11 = (pred[8,9]{0,1:T(8,128)(4,1)S(1)}, pred[8,9]{0,1:T(8,128)(4,1)}, u32[]{:S(2)}) copy-start(pred[8,9]{0,1:T(8,128)(4,1)} %constant.320) | copy-start | bytes 220 | tf_op jit(solution)/shard_map/while/body/eval_jaxpr/cond
  840.0 12.8 %copy-start.13 = (pred[8,9]{0,1:T(8,128)(4,1)S(1)}, pred[8,9]{0,1:T(8,128)(4,1)}, u32[]{:S(2)}) copy-start(pred[8,9]{0,1:T(8,128)(4,1)} %constant.325) | copy-start | bytes 220 | tf_op jit(solution)/shard_map/while/body/eval_jaxpr/cond
  858.3 5.5 copy-start.1
  859.0 4.9 collective-permute-start.5
  860.7 4.0 collective-permute-start.6
  863.9 1.9 copy-start.2
  866.0 9.1 copy-start.4
  866.0 9.1 collective-permute-start.7
  875.3 11.0 collective-permute-start
  882.3 10.3 collective-permute-start.1
  884.8 39.4 %collective-permute-start.4 = (bf16[8,128,320]{1,2,0:T(8,128)(2,1)S(1)}, bf16[8,128,320]{1,2,0:T(8,128)(2,1)}, u32[]{:S(2)}, u32[]{:S(2)}) collective-permute-start(bf16[8,128,320]{1,2,0:T(8,128)(2,1)S(1)} %fusion.186), channel_id=1, source_target_pairs={{0,192},{1,193},{2,194},{3,195},{4,196},{5,197},{6,198},{7,199},{8... | collective-permute-start | bytes 1966088 | tf_op jit(solution)/shard_map/while/body/eval_jaxpr/ppermute | solution.py:43
  894.7 64.0 %collective-permute-start.2 = (bf16[2,40960]{1,0:T(2,128)(2,1)S(1)}, bf16[2,40960]{1,0:T(2,128)(2,1)S(1)}, u32[]{:S(2)}, u32[]{:S(2)}) collective-permute-start(bf16[2,40960]{1,0:T(2,128)(2,1)S(1)} %get-tuple-element.923), channel_id=1, source_target_pairs={{0,1},{1,2},{2,3},{3,4},{4,5},{5,6},{6,7},{7,8},{8,9},{9,10},{10,1... | collective-permute-start | bytes 491528 | tf_op jit(solution)/shard_map/while/body/eval_jaxpr/ppermute | solution.py:28
  922.9 35.8 %collective-permute-start.3 = (bf16[2,40960]{1,0:T(2,128)(2,1)S(1)}, bf16[2,40960]{1,0:T(2,128)(2,1)S(1)}, u32[]{:S(2)}, u32[]{:S(2)}) collective-permute-start(bf16[2,40960]{1,0:T(2,128)(2,1)S(1)} %get-tuple-element.924), channel_id=1, source_target_pairs={{1,0},{2,1},{3,2},{4,3},{5,4},{6,5},{7,6},{8,7},{9,8},{10,9},{11,1... | collective-permute-start | bytes 491528 | tf_op jit(solution)/shard_map/while/body/eval_jaxpr/ppermute | solution.py:29
  1011.8 5.5 copy-start.1
  1012.5 4.9 collective-permute-start.5
  1014.3 4.0 collective-permute-start.6
  1017.4 1.9 copy-start.2
  1019.5 59.4 %copy-start.4 = (bf16[1,4,128,320]{2,3,1,0:T(8,128)(2,1)S(1)}, bf16[1,4,128,320]{2,3,1,0:T(8,128)(2,1)}, u32[]{:S(2)}) copy-start(bf16[1,4,128,320]{2,3,1,0:T(8,128)(2,1)} %get-tuple-element.1072) | copy-start | bytes 983044 | tf_op jit(solution)/shard_map/while
  1019.5 59.4 %collective-permute-start.7 = (bf16[2,64,640]{2,0,1:T(2,128)(2,1)S(1)}, bf16[2,64,640]{2,0,1:T(2,128)(2,1)S(1)}, u32[]{:S(2)}, u32[]{:S(2)}) collective-permute-start(bf16[2,64,640]{2,0,1:T(2,128)(2,1)S(1)} %get-tuple-element.1046), channel_id=1, source_target_pairs={{0,64},{64,128},{128,192},{1,65},{65,129},{129,193},{2,66},{66,130... | collective-permute-start | bytes 491528 | tf_op jit(solution)/shard_map/while/body/eval_jaxpr/ppermute | solution.py:43
Sparse Core Ops, SparseCore 0:
  10.8 224.0 all-gather.1
where the time goes:
time: 1120 us; the launch traced here: 1100 us
  waiting for transfers between devices  318 us (28%)
  blocking collectives  264 us (24%)
  starting transfers between devices  242 us (22%)
  local copies, waits for them, and re-layouts  146 us (13%)
  loops' own time  89.7 us (8%)
  other arithmetic  17.1 us (2%)
  between operations  13.7 us (1%)
    psum x32, blocking collectives, over_axes(): x = lax.psum(x, axis)  252 us
    all_gather x1, waiting for transfers between devices, shards(): gathered = lax.all_gather(section_packs, SPACE, axis=2, tiled=True)  226 us
    ppermute x12, starting transfers between devices, padded(): before = lax.ppermute(last, axis, up)  134 us
    ppermute x8, starting transfers between devices, passed_along(): lax.ppermute(value, axis, [(source, source + steps) for source in range(i...  92.5 us
    another operation x4, loops' own time, section_tick(): hidden_fine, hidden_coarse = lax.switch(branch_pick, branches(first_conv))  70.1 us
    ppermute x8, waiting for transfers between devices, passed_along(): lax.ppermute(value, axis, [(source, source + steps) for source in range(i...  66.3 us
    all_gather x1, local copies, waits for them, and re-layouts, shards(): gathered = lax.all_gather(section_packs, SPACE, axis=2, tiled=True)  56.7 us
    slice x4, local copies, waits for them, and re-layouts, kernel_at(): flat_pack[offset:offset + 9 * c_in * c_out].reshape(3, 3, c_in, c_out)  38.7 us
  transfers between devices with their start and end apart: 33, of which 13 were waited for; matrix products, arithmetic and copies ran while one was open for 2% of the time, Pallas kernels for 0%

commit v1 on v0

v1 whole, which is shorter than its diff:
```python
import math

import jax
import jax.numpy as jnp
import numpy as np
from jax import lax
from jax.experimental import pallas as pl
from jax.experimental.pallas import tpu as pltpu
from jax.sharding import PartitionSpec as P

F32 = jnp.float32
BF16 = jnp.bfloat16
MESH = pl.DeviceIdType.MESH
EPSILON = 1e-05
CHUNK = 1920
HALF_A = 1024
HALF_B = CHUNK - HALF_A
ROW_N = 512 * 10


def selections():
    rows = np.arange(512)
    slot, lane = rows // 16, rows % 16
    chan_fine = np.where(lane < 10, 10 * ((slot % 16) * 2 + slot // 16) + lane, -1)
    rows = np.arange(1024)
    slot, lane = rows // 16, rows % 16
    chan_wide = np.where(lane < 10, 10 * ((slot % 32) * 2 + slot // 32) + lane, -1)
    split = lambda n: np.concatenate([np.arange(0, n, 2), np.arange(1, n, 2)])
    di, di_wide = split(320), split(640)
    nat, nat_wide = np.arange(320), np.arange(640)
    eq = lambda a, b: (a[:, None] == b[None, :])
    b = np.arange(128)
    shifts = np.stack([eq(b, b + dx) for dx in (-1, 1)])
    strided = np.stack(
        [
            np.stack([eq(b, 2 * (b % 64) + dx) & (b // 64 == i)[None, :] for dx in (-1, 0, 1)])
            for i in (0, 1)
        ]
    )
    doubled = np.stack(
        [
            np.stack(
                [
                    eq(b, 64 * half + (b + dx) // 2) & ((b + dx >= 0) & (b + dx < 128))[None, :]
                    for dx in (-1, 0, 1)
                ]
            )
            for half in (0, 1)
        ]
    )

    def taps(rows_in, rows_out):
        a, c = np.arange(rows_in * 64), np.arange(rows_out * 64)
        out = []
        for dy in (0, 1, 2):
            for dx in (-1, 0, 1):
                col = c % 64 + dx
                out.append(
                    eq(a, (c // 64 + dy) * 64 + col) & ((col >= 0) & (col < 64))[None, :]
                )
        return np.stack(out)

    group = np.arange(128)
    fine_groups = np.stack(
        [eq(di // 10, group), eq(di // 20, group), eq(16 + di // 20, group)]
    )
    wide_groups = eq(nat_wide // 20, group)
    bf = lambda m: np.asarray(m, np.float32).astype(jnp.bfloat16)
    return (
        bf(eq(di, chan_fine)),
        bf(eq(nat, chan_fine)),
        bf(eq(chan_fine, di)),
        bf(eq(chan_fine, nat)),
        bf(eq(nat_wide, chan_wide)),
        bf(eq(chan_wide, nat_wide)),
        bf(eq(di, nat)),
        bf(eq(di_wide, nat_wide)),
        bf(shifts),
        bf(strided),
        bf(doubled),
        bf(taps(6, 4)),
        bf(taps(4, 2)),
        np.asarray(fine_groups, np.float32),
        np.asarray(wide_groups, np.float32),
    )


def dot(a, b):
    return jnp.dot(a, b, preferred_element_type=F32)


def activate(values, mean, rstd):
    z = (values - mean) * rstd
    return z / (1.0 + jnp.exp(-z))


def kernel(
    x_ref, w_ref, sel_di, sel_nat, exp_di, exp_nat, sel_c, exp_c, perm_x, perm_c, shifts, strided,
    doubled, taps_one, taps_two, fine_groups, wide_groups, out_ref,
    W, col, colj, sh, xr, xd, hid, skd, skn, skb, cb, tile, a3, a2, hs, acc, ud, outs, landed,
    SA, SB, HS, gather_send, gather_recv, a_send, a_recv, b_send, b_recv,
    x_send, x_recv, c_send, c_recv, k_send, k_recv, o_send, o_recv,
):
    sec = lax.axis_index("section")
    d = lax.axis_index("space")
    c = lax.rem(d, 2)
    z = lax.rem(lax.div(d, 2), 2)
    x = lax.rem(lax.div(d, 4), 4)
    y = lax.div(d, 16)
    hi, lo = lax.div(d, 8), lax.rem(d, 8)
    space = lambda y, x, z, c: ((y * 4 + x) * 2 + z) * 2 + c
    xp, xm = lax.rem(x + 1, 4), lax.rem(x + 3, 4)
    yp, ym = lax.rem(y + 1, 4), lax.rem(y + 3, 4)
    below, above = lax.rem(d + 1, 64), lax.rem(d + 63, 64)
    lo_peer = lambda k: hi * 8 + lax.rem(lo + k, 8)
    hi_peer = lambda k: lax.rem(hi + k, 8) * 8 + lo
    after, before = lax.rem(sec + 1, 4), lax.rem(sec + 3, 4)
    is_top = d == 0
    is_bottom = d == 63
    keep_top = jnp.where(is_top, 0.0, 1.0)
    keep_bottom = jnp.where(is_bottom, 0.0, 1.0)

    barrier = pltpu.get_barrier_semaphore()
    peers = [(sec, lo_peer(k)) for k in range(1, 8)] + [(sec, hi_peer(k)) for k in range(1, 8)]
    peers += [(sec, space(y, xp, z, c)), (sec, space(y, xm, z, c)), (sec, below), (sec, above)]
    for other in (after, before):
        peers += [(other, hi_peer(k)) for k in range(8)] + [(other, below), (other, above)]
    peers += [(lax.rem(sec + 2, 4), d)]
    for peer in peers:
        pl.semaphore_signal(barrier, inc=1, device_id=peer, device_id_type=MESH)

    W[c, y, x, pl.ds(pl.multiple_of(16 * z, 16), 16), :] = w_ref[...]
    pl.semaphore_wait(barrier, len(peers))

    def remote(src, dst, send, recv, peer):
        return pltpu.make_async_remote_copy(
            src_ref=src, dst_ref=dst, send_sem=send, recv_sem=recv, device_id=peer,
            device_id_type=MESH,
        )

    def to_message(mean, deviation):
        return jnp.concatenate([mean, deviation, jnp.zeros((6, 128), F32)], axis=0)

    def combined(messages, count):
        means = messages[:, 0:1, :]
        mean = jnp.sum(means, axis=0) * 0.125
        spread = jnp.sum(jnp.square(means - mean[None]), axis=0) * count
        return mean, jnp.sum(messages[:, 1:2, :], axis=0) + spread

    def part_sums(blocks, groups, count, weight=None):
        total = blocks[0] if weight is None else blocks[0] * weight
        for block in blocks[1:]:
            total = total + block
        channel = jnp.sum(total, axis=1, keepdims=True)
        mean = jnp.sum(groups * channel, axis=0, keepdims=True) * (1.0 / count)
        own = jnp.sum(groups * mean, axis=1, keepdims=True)
        squares = None
        for block in blocks:
            off = jnp.square(block - own)
            off = off if weight is None else off * weight
            squares = off if squares is None else squares + off
        channel = jnp.sum(squares, axis=1, keepdims=True)
        return mean, jnp.sum(groups * channel, axis=0, keepdims=True)

    def first_copies(e):
        return [
            remote(SA.at[e, 0], SA.at[e, k], a_send.at[e, k], a_recv.at[e, k], (sec, lo_peer(k)))
            for k in range(1, 8)
        ]

    def start_first(e, mean, deviation):
        SA[e, 0] = to_message(mean, deviation)
        for copy in first_copies(e):
            copy.start()

    def finish_first(e, count):
        for copy in first_copies(e):
            copy.wait()
        return combined(SA[e], count)

    def second_copies(e):
        return [
            remote(SB.at[e, 0], SB.at[e, k], b_send.at[e, k], b_recv.at[e, k], (sec, hi_peer(k)))
            for k in range(1, 8)
        ]

    def scale_rows(e, count):
        mean, squares = combined(SB[e], 8 * count)
        return mean, lax.rsqrt(squares * (1.0 / (64 * count)) + EPSILON)

    def start_second(e, count):
        mean, deviation = finish_first(e, count)
        SB[e, 0] = to_message(mean, deviation)
        for copy in second_copies(e):
            copy.start()

    def finish_second(e, count):
        for copy in second_copies(e):
            copy.wait()
        return scale_rows(e, count)

    def exchanged(e, mean, deviation, count):
        start_first(e, mean, deviation)
        start_second(e, count)
        return finish_second(e, count)

    def columns(groups, rows):
        return [jnp.sum(groups * row, axis=1, keepdims=True) for row in rows]

    def across_copies():
        return [
            remote(HS, SB.at[2, k], b_send.at[2, k], b_recv.at[2, k], (after, hi_peer(k)))
            for k in range(8)
        ]

    def tile_copies():
        return [
            remote(tile, cb.at[slot], c_send.at[slot], c_recv.at[slot], (after, peer))
            for slot, peer in ((1, d), (0, below), (2, above))
        ]

    def skip_copies():
        return [
            remote(skd.at[lax_rows(1, 4)], skb.at[lax_rows(2, 4)], k_send.at[0], k_recv.at[0], (before, d)),
            remote(skd.at[lax_rows(3, 2)], skb.at[lax_rows(0, 2)], k_send.at[1], k_recv.at[1], (before, below)),
            remote(skd.at[lax_rows(1, 2)], skb.at[lax_rows(6, 2)], k_send.at[2], k_recv.at[2], (before, above)),
        ]

    def lax_rows(start, size):
        return pl.ds(start, size)

    def hand_over(count):
        for copy in tile_copies():
            copy.start()
        mean, deviation = part_sums([tile[...].astype(F32)], wide_groups[...], count)
        start_first(2, mean, deviation)
        HS[...] = to_message(*finish_first(2, count))
        for copy in across_copies():
            copy.start()
        for copy in tile_copies() + across_copies():
            copy.wait_send()

    def take_over():
        for copy in tile_copies() + across_copies():
            copy.wait_recv()

    chunks = jnp.where(sec == 0, 3, jnp.where(sec == 3, 4, 6))

    def gather_copies(stage, k):
        lane = lambda off, size: pl.ds(pl.multiple_of(k * CHUNK + off, 128), size)
        whole, part_a, part_b = lane(0, CHUNK), lane(0, HALF_A), lane(HALF_A, HALF_B)
        to_xp, to_xm = space(y, xp, z, c), space(y, xm, z, c)
        to_yp, to_ym = space(yp, x, z, c), space(ym, x, z, c)
        all32, first, second = pl.ds(0, 32), pl.ds(0, 16), pl.ds(16, 16)
        every, low, high = pl.ds(0, 4), pl.ds(0, 2), pl.ds(2, 2)
        if stage == 0:
            moves = [((c, y, x, pl.ds(pl.multiple_of(16 * z, 16), 16), whole), space(y, x, 1 - z, c))]
        elif stage == 1:
            a, b = (c, y, x, all32, part_a), (c, y, x, all32, part_b)
            moves = [(a, to_xp), (a, to_xm), (b, to_yp), (b, to_ym)]
        elif stage == 2:
            moves = [
                ((c, y, xm, first, part_a), to_xp),
                ((c, y, xp, second, part_a), to_xm),
                ((c, ym, x, first, part_b), to_yp),
                ((c, yp, x, second, part_b), to_ym),
            ]
        elif stage == 3:
            a, b = (c, y, every, all32, part_a), (c, every, x, all32, part_b)
            moves = [(a, to_yp), (a, to_ym), (b, to_xp), (b, to_xm)]
        elif stage == 4:
            moves = [
                ((c, ym, low, all32, part_a), to_yp),
                ((c, yp, high, all32, part_a), to_ym),
                ((c, low, xm, all32, part_b), to_xp),
                ((c, high, xp, all32, part_b), to_xm),
            ]
        else:
            moves = [((c, every, every, all32, whole), space(y, x, z, 1 - c))]
        first_id = (0, 1, 5, 9, 13, 17)[stage]
        return [
            remote(
                W.at[where], W.at[where], gather_send.at[first_id + i, k],
                gather_recv.at[first_id + i, k], (sec, peer),
            )
            for i, (where, peer) in enumerate(moves)
        ]

    def gather():
        def step(t, carry):
            for stage in range(7):
                k = t - stage

                @pl.when((k >= 0) & (k < chunks))
                def _():
                    if stage > 0:
                        for copy in gather_copies(stage - 1, k):
                            copy.wait_recv()
                    if stage < 6:
                        for copy in gather_copies(stage, k):
                            copy.start()

            return carry

        lax.fori_loop(0, chunks + 6, step, 0)

    def gather_end():
        def step(k, carry):
            for stage in range(6):
                for copy in gather_copies(stage, k):
                    copy.wait_send()
            return carry

        lax.fori_loop(0, chunks, step, 0)

    def put_shifted(index, base, values):
        size = values.shape[0]
        sh[1, index, base : base + size, :] = values
        sh[0, index, base : base + size, :] = dot(values, shifts[0]).astype(BF16)
        sh[2, index, base : base + size, :] = dot(values, shifts[1]).astype(BF16)

    def fine_conv(pairs, pieces, per_tap, lead, lane_start, depth, source_row, use):
        taps = 9 * per_tap
        for p in range(2):
            if lead:
                col[p, 0:lead, :] = jnp.zeros((lead, 256), BF16)
            if lead + taps < depth:
                col[p, lead + taps : depth, :] = jnp.zeros((depth - lead - taps, 256), BF16)

        def pair(q, carry):
            for p in range(2):
                for dy in range(3):
                    for j in range(2):
                        row = source_row(q, j + dy)
                        for dx in range(3):
                            at = lead + (dy * 3 + dx) * per_tap
                            for to, start, size in pieces(p):
                                col[p, at + to : at + to + size, 128 * j : 128 * j + 128] = sh[
                                    dx, row, start : start + size, :
                                ]
            use(q, weighted(lane_start, depth, col))
            return carry

        lax.fori_loop(0, pairs, pair, 0)

    def weighted(lane_start, depth, source):
        total = None
        for p in range(2):
            kernels = W[:, 2 * p : 2 * p + 2, :, :, lane_start : lane_start + depth]
            made = dot(kernels.reshape(512, depth), source[p, 0:depth, :])
            total = made if total is None else total + made
        return total

    narrow_pieces = lambda p: [(0, 160 * p, 160)]
    wide_pieces = lambda p: [(0, 320 * p, 320)]
    joined_pieces = lambda p: [(0, 160 * p, 160), (160, 320 + 160 * p, 160)]
    follow = lambda q, off: 2 * q + off
    narrow_scale = 1.0 / math.sqrt(9 * 320)
    wide_scale = 1.0 / math.sqrt(9 * 640)

    def row_kept(row):
        return jnp.where(row < 0, keep_top, jnp.where(row > 3, keep_bottom, 1.0))

    def activate_rows(source, count, first_row, mean, rstd):
        def one(r, carry):
            values = activate(source[r].astype(F32), mean, rstd) * row_kept(r + first_row)
            put_shifted(r, 0, values.astype(BF16))
            return carry

        lax.fori_loop(0, count, one, 0)

    @pl.when(sec == 0)
    def _():
        x_copies = [
            remote(x_ref.at[pl.ds(1, 3)], xr.at[pl.ds(0, 3)], x_send.at[0], x_recv.at[0], (0, below)),
            remote(x_ref.at[pl.ds(0, 2)], xr.at[pl.ds(7, 2)], x_send.at[1], x_recv.at[1], (0, above)),
        ]
        for copy in x_copies:
            copy.start()
        for r in range(4):
            xr[3 + r] = x_ref[r]
        xr[9] = jnp.zeros((320, 128), BF16)

        def permute(r, carry):
            xd[r] = dot(perm_x[...], xr[r]).astype(BF16)
            return carry

        lax.fori_loop(3, 7, permute, 0)
        groups = fine_groups[0]
        start_first(0, *part_sums([xd[r].astype(F32) for r in range(3, 7)], groups, ROW_N))
        gather()
        start_second(0, ROW_N)
        for copy in x_copies:
            copy.wait()
        lax.fori_loop(0, 3, permute, 0)
        lax.fori_loop(7, 10, permute, 0)
        mean, rstd = columns(groups, finish_second(0, ROW_N))
        activate_rows(xd, 10, -3, mean, rstd)

        def keep_hidden(q, made):
            rounded = (made * narrow_scale).astype(BF16)
            packed = dot(sel_di[...], rounded).astype(BF16)
            hid[2 * q] = packed[:, 0:128]
            hid[2 * q + 1] = packed[:, 128:256]

        fine_conv(4, narrow_pieces, 160, 0, 0, 1536, follow, keep_hidden)
        sums = part_sums([hid[r].astype(F32) for r in range(2, 6)], groups, ROW_N)
        mean, rstd = columns(groups, exchanged(1, *sums, ROW_N))
        activate_rows(hid, 8, -2, mean, rstd)

        def keep_skip(q, made):
            for j in range(2):
                own = dot(exp_di[...], xd[2 * q + j + 2])
                rounded = (own + made[:, 128 * j : 128 * j + 128] * narrow_scale).astype(BF16)
                skd[2 * q + j] = dot(sel_di[...], rounded).astype(BF16)
                skn[2 * q + j] = dot(sel_nat[...], rounded).astype(BF16)

        fine_conv(3, narrow_pieces, 160, 32, 1408, 1536, follow, keep_skip)
        for copy in skip_copies():
            copy.start()
        skn[0] = (skn[0].astype(F32) * keep_top).astype(BF16)
        col[0, 0:64, 0:128] = jnp.zeros((64, 128), BF16)
        for dy in range(3):
            for dx in range(3):
                at = 64 + (dy * 3 + dx) * 320
                made = dot(skn[dy], strided[0, dx]) + dot(skn[2 + dy], strided[1, dx])
                col[0, at : at + 320, 0:128] = made.astype(BF16)
        made = dot(W[:, :, :, :, 2816:5760].reshape(1024, 2944), col[0, :, 0:128])
        rounded = (made * narrow_scale).astype(BF16)
        tile[...] = dot(sel_c[...], rounded).astype(BF16)
        hand_over(128 * 20)
        for copy in skip_copies():
            copy.wait_send()

    @pl.when((sec == 1) | (sec == 2))
    def _():
        gather()
        take_over()
        count = 128 * 20
        groups = wide_groups[...]
        mean, rstd = columns(groups, scale_rows(2, count))
        for i in range(3):
            values = activate(cb[i].astype(F32), mean, rstd)
            values = values * (keep_top, 1.0, keep_bottom)[i]
            a3[:, 128 * i : 128 * i + 128] = values.astype(BF16)

        acc[...] = jnp.zeros((1024, 256), F32)

        def first_tap(t, carry):
            moved = dot(a3[...], taps_one[t]).astype(BF16)
            lanes = pl.ds(pl.multiple_of(t * 640, 128), 640)
            acc[...] += dot(W[:, :, :, :, lanes].reshape(1024, 640), moved)
            return carry

        lax.fori_loop(0, 9, first_tap, 0)
        rounded = (acc[...] * wide_scale).astype(BF16)
        hs[...] = dot(sel_c[...], rounded)
        column = lax.broadcasted_iota(jnp.int32, (1, 256), 1)
        inner = jnp.where((column >= 64) & (column < 192), 1.0, 0.0)
        kept = jnp.where(column < 64, keep_top, jnp.where(column >= 192, keep_bottom, 1.0))
        sums = part_sums([hs[...]], groups, count, inner)
        mean, rstd = columns(groups, exchanged(3, *sums, count))
        a2[...] = (activate(hs[...], mean, rstd) * kept).astype(BF16)
        acc[:, 0:128] = jnp.zeros((1024, 128), F32)

        def second_tap(t, carry):
            moved = dot(a2[...], taps_two[t]).astype(BF16)
            lanes = pl.ds(pl.multiple_of(5760 + t * 640, 128), 640)
            acc[:, 0:128] += dot(W[:, :, :, :, lanes].reshape(1024, 640), moved)
            return carry

        lax.fori_loop(0, 9, second_tap, 0)
        own = dot(exp_c[...], cb[1])
        rounded = (own + acc[:, 0:128] * wide_scale).astype(BF16)
        tile[...] = dot(sel_c[...], rounded).astype(BF16)
        hand_over(count)

    def out_copies(sections=range(3)):
        return [
            remote(
                outs.at[pl.ds(0, 4), pl.ds(32 * t, 32)], landed, o_send.at[t], o_recv.at[0], (t, d)
            )
            for t in sections
        ]

    @pl.when(sec == 3)
    def _():
        gather()
        for copy in skip_copies():
            copy.wait_recv()
        take_over()
        for i in range(3):
            moved = dot(perm_c[...], cb[i]) * (keep_top, 1.0, keep_bottom)[i]
            moved = moved.astype(BF16)
            for half in range(2):
                for dx in range(3):
                    sh[dx, 2 * i + half] = dot(moved, doubled[half, dx]).astype(BF16)

        def keep_upper(q, made):
            rounded = (made * wide_scale).astype(BF16)
            packed = dot(sel_di[...], rounded).astype(BF16)
            ud[2 * q] = packed[:, 0:128]
            ud[2 * q + 1] = packed[:, 128:256]

        half_row = lambda q, off: q + (off + 1) // 2
        fine_conv(4, wide_pieces, 320, 0, 0, 2944, half_row, keep_upper)
        groups_u, groups_s = fine_groups[1], fine_groups[2]
        mean_u, dev_u = part_sums([ud[r].astype(F32) for r in range(2, 6)], groups_u, 2 * ROW_N)
        mean_s, dev_s = part_sums([skb[r].astype(F32) for r in range(2, 6)], groups_s, 2 * ROW_N)
        rows = exchanged(4, mean_u + mean_s, dev_u + dev_s, 2 * ROW_N)
        mean_u, rstd_u = columns(groups_u, rows)
        mean_s, rstd_s = columns(groups_s, rows)

        def joined_row(r, carry):
            kept = row_kept(r - 2)
            upper = activate(ud[r].astype(F32), mean_u, rstd_u) * kept
            put_shifted(r, 0, upper.astype(BF16))
            lower = activate(skb[r].astype(F32), mean_s, rstd_s) * kept
            put_shifted(r, 320, lower.astype(BF16))
            return carry

        lax.fori_loop(0, 8, joined_row, 0)

        def keep_hidden(q, made):
            rounded = (made * wide_scale).astype(BF16)
            packed = dot(sel_di[...], rounded).astype(BF16)
            hid[2 * q] = packed[:, 0:128]
            hid[2 * q + 1] = packed[:, 128:256]

        fine_conv(3, joined_pieces, 320, 64, 2816, 2944, follow, keep_hidden)
        groups = fine_groups[0]
        sums = part_sums([hid[r].astype(F32) for r in range(1, 5)], groups, ROW_N)
        mean, rstd = columns(groups, exchanged(5, *sums, ROW_N))
        activate_rows(hid, 6, -1, mean, rstd)
        for p in range(2):
            colj[p, 0:32, :] = jnp.zeros((32, 256), BF16)
            colj[p, 352:384, :] = jnp.zeros((32, 256), BF16)

        def keep_output(q, made):
            for p in range(2):
                for j in range(2):
                    px = slice(128 * j, 128 * j + 128)
                    colj[p, 32:192, px] = ud[2 * q + j + 2, 160 * p : 160 * p + 160, :]
                    colj[p, 192:352, px] = skb[2 * q + j + 2, 160 * p : 160 * p + 160, :]
            straight = weighted(7168, 384, colj)
            total = made * narrow_scale + straight * (1.0 / math.sqrt(640))
            rounded = total.astype(BF16)
            for j in range(2):
                flipped = lax.dot_general(
                    rounded[:, 128 * j : 128 * j + 128], exp_nat[...], (((0,), (0,)), ((), ())),
                    preferred_element_type=F32,
                )
                outs[2 * q + j] = flipped.astype(BF16)

        fine_conv(2, narrow_pieces, 160, 0, 5760, 1536, follow, keep_output)
        for copy in out_copies():
            copy.start()
        out_ref[...] = outs[:, 96:128, :]
        for copy in out_copies():
            copy.wait_send()

    @pl.when(sec < 3)
    def _():
        for copy in out_copies((0,)):
            copy.wait_recv()
        out_ref[...] = landed[...]

    gather_end()


def shards(features, section_packs):
    fields = jnp.swapaxes(features[0], 1, 2)
    packs = jnp.pad(jnp.swapaxes(section_packs[0], 0, 1), ((0, 6), (0, 0)))
    tables = selections()
    dma = pltpu.SemaphoreType.DMA
    scratch = [
        pltpu.VMEM((2, 4, 4, 32, 11520), BF16),
        pltpu.VMEM((2, 2944, 256), BF16),
        pltpu.VMEM((2, 384, 256), BF16),
        pltpu.VMEM((3, 10, 640, 128), BF16),
        pltpu.VMEM((10, 320, 128), BF16),
        pltpu.VMEM((10, 320, 128), BF16),
        pltpu.VMEM((8, 320, 128), BF16),
        pltpu.VMEM((6, 320, 128), BF16),
        pltpu.VMEM((6, 320, 128), BF16),
        pltpu.VMEM((8, 320, 128), BF16),
        pltpu.VMEM((3, 640, 128), BF16),
        pltpu.VMEM((640, 128), BF16),
        pltpu.VMEM((640, 384), BF16),
        pltpu.VMEM((640, 256), BF16),
        pltpu.VMEM((640, 256), F32),
        pltpu.VMEM((1024, 256), F32),
        pltpu.VMEM((8, 320, 128), BF16),
        pltpu.VMEM((4, 128, 320), BF16),
        pltpu.VMEM((4, 32, 320), BF16),
        pltpu.VMEM((6, 8, 8, 128), F32),
        pltpu.VMEM((6, 8, 8, 128), F32),
        pltpu.VMEM((8, 128), F32),
        dma((18, 6)), dma((18, 6)),
        dma((6, 8)), dma((6, 8)), dma((6, 8)), dma((6, 8)),
        dma((2,)), dma((2,)), dma((3,)), dma((3,)), dma((3,)), dma((3,)), dma((3,)), dma((1,)),
    ]
    vmem = pl.BlockSpec(memory_space=pltpu.VMEM)
    out = pl.pallas_call(
        kernel,
        out_shape=jax.ShapeDtypeStruct((4, 32, 320), BF16),
        in_specs=[vmem] * (2 + len(tables)),
        out_specs=vmem,
        scratch_shapes=scratch,
        compiler_params=pltpu.CompilerParams(
            collective_id=0, has_side_effects=True, vmem_limit_bytes=62 * 1024 * 1024
        ),
        cost_estimate=pl.CostEstimate(
            flops=12_000_000_000, bytes_accessed=30_000_000, transcendentals=2_000_000
        ),
    )(fields, packs, *tables)
    return out[None]


def solution(mesh):
    return jax.shard_map(
        shards,
        mesh=mesh,
        in_specs=(P(None, "space", None, None), P("section", None, "space")),
        out_specs=P(None, "space", "section", None),
        check_vma=False,
    )
```

time: 1120 us -> 277 us (0.25); the launches traced: 1100 us -> 277 us
  waiting for transfers between devices: 318 us -> 0 us
  Pallas kernels: 0 us -> 273 us
  blocking collectives: 264 us -> 0 us
  starting transfers between devices: 242 us -> 0 us
  local copies, waits for them, and re-layouts: 146 us -> 3.29 us
  loops' own time: 89.7 us -> 0 us
  other arithmetic: 17.1 us -> 0 us
  between operations: 13.7 us -> 0.01 us
    pallas_call x0 -> x1, Pallas kernels: none -> 273 us  [shards(): pl.pallas_call(kernel, out_shape=jax.ShapeDtypeStruct((4, 32, 320), BF16)...]
    psum x32 -> x0, blocking collectives: 252 us -> none  [over_axes(): x = lax.psum(x, axis)]
    ppermute x32 -> x0, starting transfers between devices: 242 us -> none  [the longest x12 134 us: padded(): before = lax.ppermute(last, axis, up)]
    all_gather x1 -> x0, waiting for transfers between devices: 226 us -> none  [shards(): gathered = lax.all_gather(section_packs, SPACE, axis=2, tiled=True)]
    ppermute x32 -> x0, waiting for transfers between devices: 91.5 us -> none  [the longest x8 66.3 us: passed_along(): lax.ppermute(value, axis, [(source, source + steps) for source in range(i...]
    another operation x25 -> x0, loops' own time: 89.7 us -> none  [the longest x4 70.1 us: section_tick(): hidden_fine, hidden_coarse = lax.switch(branch_pick, branches(first_conv))]
    all_gather x1 -> x0, local copies, waits for them, and re-layouts: 56.7 us -> none  [shards(): gathered = lax.all_gather(section_packs, SPACE, axis=2, tiled=True)]
    slice x36 -> x0, local copies, waits for them, and re-layouts: 46.4 us -> none  [the longest x4 38.7 us: kernel_at(): flat_pack[offset:offset + 9 * c_in * c_out].reshape(3, 3, c_in, c_out)]
  transfers between devices with their start and end apart: 33 -> 0, of which waited for: 13 -> 0; matrix products, arithmetic and copies ran while one was open for 2% -> 0% of each run, Pallas kernels for 0% -> 0%
where the time goes in v1:
time: 277 us
  Pallas kernels  273 us (99%)
  local copies, waits for them, and re-layouts  3.29 us (1%)
    pallas_call x1, Pallas kernels, shards(): pl.pallas_call(kernel, out_shape=jax.ShapeDtypeStruct((4, 32, 320), BF16)...  273 us

profile of v1, /device:TPU:64, one launch (start us, length us, event | category | flops | bytes accessed | tf_op | source)
XLA Modules:
  0.0 276.6 jit_solution(5504323793415077502)
XLA Ops:
  0.0 1.7 pad.4.w_ref
  1.7 273.3 %shard_map.163 = bf16[4,32,320]{2,1,0:T(8,128)(2,1)} custom-call(bf16[4,320,128]{2,1,0:T(8,128)(2,1)} %bitcast.9, bf16[16,11520]{1,0:T(8,128)(2,1)} %pad.4.w_ref, bf16[320,512]{1,0:T(8,128)(2,1)} %constant.33.clone.sel_di, bf16[320,512]{1,0:T(8,128)(2,1)} %constant.34.clone.sel_nat, bf16[512,320]{1,0:T(8,128)(2,1)} %constant.35.clone.exp_di, ...), custom_call_target="tpu_custom_call" | custom-call | flops 12000000000 | bytes 30000000 | tf_op jit(solution)/shard_map/pallas_call | solution.py:604
  275.0 1.5 copy.19

commit v2 on v1

--- a/solution.py
+++ b/solution.py
@@ -12,10 +12,11 @@
 BF16 = jnp.bfloat16
 MESH = pl.DeviceIdType.MESH
 EPSILON = 1e-05
-CHUNK = 1920
-HALF_A = 1024
+CHUNK = 1536
+HALF_A = 768
 HALF_B = CHUNK - HALF_A
 ROW_N = 512 * 10
+LANES = 8 * CHUNK
 
 
 def selections():
@@ -97,8 +98,8 @@
 def kernel(
     x_ref, w_ref, sel_di, sel_nat, exp_di, exp_nat, sel_c, exp_c, perm_x, perm_c, shifts, strided,
     doubled, taps_one, taps_two, fine_groups, wide_groups, out_ref,
-    W, col, colj, sh, xr, xd, hid, skd, skn, skb, cb, tile, a3, a2, hs, acc, ud, outs, landed,
-    SA, SB, HS, gather_send, gather_recv, a_send, a_recv, b_send, b_recv,
+    W, col, colw, colj, sh, xr, xd, hid, skd, skn, skb, cb, tile, a3, a2, hs, acc, ud, outs, landed,
+    SA, HS, HR, gather_send, gather_recv, a_send, a_recv, b_send, b_recv,
     x_send, x_recv, c_send, c_recv, k_send, k_recv, o_send, o_recv,
 ):
     sec = lax.axis_index("section")
@@ -107,13 +108,10 @@
     z = lax.rem(lax.div(d, 2), 2)
     x = lax.rem(lax.div(d, 4), 4)
     y = lax.div(d, 16)
-    hi, lo = lax.div(d, 8), lax.rem(d, 8)
     space = lambda y, x, z, c: ((y * 4 + x) * 2 + z) * 2 + c
     xp, xm = lax.rem(x + 1, 4), lax.rem(x + 3, 4)
     yp, ym = lax.rem(y + 1, 4), lax.rem(y + 3, 4)
     below, above = lax.rem(d + 1, 64), lax.rem(d + 63, 64)
-    lo_peer = lambda k: hi * 8 + lax.rem(lo + k, 8)
-    hi_peer = lambda k: lax.rem(hi + k, 8) * 8 + lo
     after, before = lax.rem(sec + 1, 4), lax.rem(sec + 3, 4)
     is_top = d == 0
     is_bottom = d == 63
@@ -121,16 +119,21 @@
     keep_bottom = jnp.where(is_bottom, 0.0, 1.0)
 
     barrier = pltpu.get_barrier_semaphore()
-    peers = [(sec, lo_peer(k)) for k in range(1, 8)] + [(sec, hi_peer(k)) for k in range(1, 8)]
-    peers += [(sec, space(y, xp, z, c)), (sec, space(y, xm, z, c)), (sec, below), (sec, above)]
+    peers = [(lax.rem(sec + 2, 4), d)]
     for other in (after, before):
-        peers += [(other, hi_peer(k)) for k in range(8)] + [(other, below), (other, above)]
-    peers += [(lax.rem(sec + 2, 4), d)]
+        peers += [(other, d), (other, below), (other, above)]
     for peer in peers:
         pl.semaphore_signal(barrier, inc=1, device_id=peer, device_id_type=MESH)
 
+    def greet(k, carry):
+        peer = (sec, lax.rem(d + k, 64))
+        pl.semaphore_signal(barrier, inc=1, device_id=peer, device_id_type=MESH)
+        return carry
+
+    lax.fori_loop(1, 64, greet, 0)
+
     W[c, y, x, pl.ds(pl.multiple_of(16 * z, 16), 16), :] = w_ref[...]
-    pl.semaphore_wait(barrier, len(peers))
+    pl.semaphore_wait(barrier, len(peers) + 63)
 
     def remote(src, dst, send, recv, peer):
         return pltpu.make_async_remote_copy(
@@ -138,14 +141,12 @@
             device_id_type=MESH,
         )
 
-    def to_message(mean, deviation):
-        return jnp.concatenate([mean, deviation, jnp.zeros((6, 128), F32)], axis=0)
-
     def combined(messages, count):
         means = messages[:, 0:1, :]
-        mean = jnp.sum(means, axis=0) * 0.125
+        mean = jnp.sum(means, axis=0) * (1.0 / 64)
         spread = jnp.sum(jnp.square(means - mean[None]), axis=0) * count
-        return mean, jnp.sum(messages[:, 1:2, :], axis=0) + spread
+        squares = jnp.sum(messages[:, 1:2, :], axis=0) + spread
+        return mean, lax.rsqrt(squares * (1.0 / (64 * count)) + EPSILON)
 
     def part_sums(blocks, groups, count, weight=None):
         total = blocks[0] if weight is None else blocks[0] * weight
@@ -162,56 +163,30 @@
         channel = jnp.sum(squares, axis=1, keepdims=True)
         return mean, jnp.sum(groups * channel, axis=0, keepdims=True)
 
-    def first_copies(e):
-        return [
-            remote(SA.at[e, 0], SA.at[e, k], a_send.at[e, k], a_recv.at[e, k], (sec, lo_peer(k)))
-            for k in range(1, 8)
-        ]
-
-    def start_first(e, mean, deviation):
-        SA[e, 0] = to_message(mean, deviation)
-        for copy in first_copies(e):
-            copy.start()
-
-    def finish_first(e, count):
-        for copy in first_copies(e):
-            copy.wait()
+    def start_exchange(e, mean, deviation):
+        SA[e, 0] = jnp.concatenate([mean, deviation], axis=0)
+
+        def one(k, carry):
+            peer = (sec, lax.rem(d + k, 64))
+            remote(SA.at[e, 0], SA.at[e, k], a_send.at[e], a_recv.at[e], peer).start()
+            return carry
+
+        lax.fori_loop(1, 64, one, 0)
+
+    def finish_exchange(e, count):
+        others = SA.at[e, pl.ds(1, 63)]
+        remote(others, others, a_send.at[e], a_recv.at[e], (sec, below)).wait()
         return combined(SA[e], count)
 
-    def second_copies(e):
-        return [
-            remote(SB.at[e, 0], SB.at[e, k], b_send.at[e, k], b_recv.at[e, k], (sec, hi_peer(k)))
-            for k in range(1, 8)
-        ]
-
-    def scale_rows(e, count):
-        mean, squares = combined(SB[e], 8 * count)
-        return mean, lax.rsqrt(squares * (1.0 / (64 * count)) + EPSILON)
-
-    def start_second(e, count):
-        mean, deviation = finish_first(e, count)
-        SB[e, 0] = to_message(mean, deviation)
-        for copy in second_copies(e):
-            copy.start()
-
-    def finish_second(e, count):
-        for copy in second_copies(e):
-            copy.wait()
-        return scale_rows(e, count)
-
     def exchanged(e, mean, deviation, count):
-        start_first(e, mean, deviation)
-        start_second(e, count)
-        return finish_second(e, count)
+        start_exchange(e, mean, deviation)
+        return finish_exchange(e, count)
 
     def columns(groups, rows):
         return [jnp.sum(groups * row, axis=1, keepdims=True) for row in rows]
 
-    def across_copies():
-        return [
-            remote(HS, SB.at[2, k], b_send.at[2, k], b_recv.at[2, k], (after, hi_peer(k)))
-            for k in range(8)
-        ]
+    def across_copy():
+        return remote(HS, HR, b_send.at[0], b_recv.at[0], (after, d))
 
     def tile_copies():
         return [
@@ -233,18 +208,16 @@
         for copy in tile_copies():
             copy.start()
         mean, deviation = part_sums([tile[...].astype(F32)], wide_groups[...], count)
-        start_first(2, mean, deviation)
-        HS[...] = to_message(*finish_first(2, count))
-        for copy in across_copies():
-            copy.start()
-        for copy in tile_copies() + across_copies():
+        HS[...] = jnp.concatenate(exchanged(2, mean, deviation, count), axis=0)
+        across_copy().start()
+        for copy in tile_copies() + [across_copy()]:
             copy.wait_send()
 
     def take_over():
-        for copy in tile_copies() + across_copies():
+        for copy in tile_copies() + [across_copy()]:
             copy.wait_recv()
 
-    chunks = jnp.where(sec == 0, 3, jnp.where(sec == 3, 4, 6))
+    chunks = jnp.where(sec == 0, 4, jnp.where(sec == 3, 5, 8))
 
     def gather_copies(stage, k):
         lane = lambda off, size: pl.ds(pl.multiple_of(k * CHUNK + off, 128), size)
@@ -286,7 +259,7 @@
             for i, (where, peer) in enumerate(moves)
         ]
 
-    def gather():
+    def gather(first, last):
         def step(t, carry):
             for stage in range(7):
                 k = t - stage
@@ -302,7 +275,7 @@
 
             return carry
 
-        lax.fori_loop(0, chunks + 6, step, 0)
+        lax.fori_loop(first, last, step, 0)
 
     def gather_end():
         def step(k, carry):
@@ -387,14 +360,13 @@
 
         lax.fori_loop(3, 7, permute, 0)
         groups = fine_groups[0]
-        start_first(0, *part_sums([xd[r].astype(F32) for r in range(3, 7)], groups, ROW_N))
-        gather()
-        start_second(0, ROW_N)
+        start_exchange(0, *part_sums([xd[r].astype(F32) for r in range(3, 7)], groups, ROW_N))
+        gather(0, 7)
         for copy in x_copies:
             copy.wait()
         lax.fori_loop(0, 3, permute, 0)
         lax.fori_loop(7, 10, permute, 0)
-        mean, rstd = columns(groups, finish_second(0, ROW_N))
+        mean, rstd = columns(groups, finish_exchange(0, ROW_N))
         activate_rows(xd, 10, -3, mean, rstd)
 
         def keep_hidden(q, made):
@@ -404,6 +376,7 @@
             hid[2 * q + 1] = packed[:, 128:256]
 
         fine_conv(4, narrow_pieces, 160, 0, 0, 1536, follow, keep_hidden)
+        gather(7, 8)
         sums = part_sums([hid[r].astype(F32) for r in range(2, 6)], groups, ROW_N)
         mean, rstd = columns(groups, exchanged(1, *sums, ROW_N))
         activate_rows(hid, 8, -2, mean, rstd)
@@ -418,6 +391,7 @@
         fine_conv(3, narrow_pieces, 160, 32, 1408, 1536, follow, keep_skip)
         for copy in skip_copies():
             copy.start()
+        gather(8, 10)
         skn[0] = (skn[0].astype(F32) * keep_top).astype(BF16)
         col[0, 0:64, 0:128] = jnp.zeros((64, 128), BF16)
         for dy in range(3):
@@ -434,25 +408,22 @@
 
     @pl.when((sec == 1) | (sec == 2))
     def _():
-        gather()
+        gather(0, chunks + 6)
         take_over()
         count = 128 * 20
         groups = wide_groups[...]
-        mean, rstd = columns(groups, scale_rows(2, count))
+        mean, rstd = columns(groups, [HR[0:1, :], HR[1:2, :]])
         for i in range(3):
             values = activate(cb[i].astype(F32), mean, rstd)
             values = values * (keep_top, 1.0, keep_bottom)[i]
             a3[:, 128 * i : 128 * i + 128] = values.astype(BF16)
 
-        acc[...] = jnp.zeros((1024, 256), F32)
-
-        def first_tap(t, carry):
-            moved = dot(a3[...], taps_one[t]).astype(BF16)
-            lanes = pl.ds(pl.multiple_of(t * 640, 128), 640)
-            acc[...] += dot(W[:, :, :, :, lanes].reshape(1024, 640), moved)
-            return carry
-
-        lax.fori_loop(0, 9, first_tap, 0)
+        for t in range(9):
+            colw[640 * t : 640 * t + 640, :] = dot(a3[...], taps_one[t]).astype(BF16)
+        for i in range(3):
+            lanes = slice(1920 * i, 1920 * i + 1920)
+            made = dot(W[:, :, :, :, lanes].reshape(1024, 1920), colw[lanes, :])
+            acc[...] = made if i == 0 else acc[...] + made
         rounded = (acc[...] * wide_scale).astype(BF16)
         hs[...] = dot(sel_c[...], rounded)
         column = lax.broadcasted_iota(jnp.int32, (1, 256), 1)
@@ -461,15 +432,13 @@
         sums = part_sums([hs[...]], groups, count, inner)
         mean, rstd = columns(groups, exchanged(3, *sums, count))
         a2[...] = (activate(hs[...], mean, rstd) * kept).astype(BF16)
-        acc[:, 0:128] = jnp.zeros((1024, 128), F32)
-
-        def second_tap(t, carry):
-            moved = dot(a2[...], taps_two[t]).astype(BF16)
-            lanes = pl.ds(pl.multiple_of(5760 + t * 640, 128), 640)
-            acc[:, 0:128] += dot(W[:, :, :, :, lanes].reshape(1024, 640), moved)
-            return carry
-
-        lax.fori_loop(0, 9, second_tap, 0)
+        for t in range(9):
+            colw[640 * t : 640 * t + 640, 0:128] = dot(a2[...], taps_two[t]).astype(BF16)
+        for i in range(3):
+            lanes = slice(5760 + 1920 * i, 5760 + 1920 * i + 1920)
+            source = colw[1920 * i : 1920 * i + 1920, 0:128]
+            made = dot(W[:, :, :, :, lanes].reshape(1024, 1920), source)
+            acc[:, 0:128] = made if i == 0 else acc[:, 0:128] + made
         own = dot(exp_c[...], cb[1])
         rounded = (own + acc[:, 0:128] * wide_scale).astype(BF16)
         tile[...] = dot(sel_c[...], rounded).astype(BF16)
@@ -485,7 +454,7 @@
 
     @pl.when(sec == 3)
     def _():
-        gather()
+        gather(0, chunks + 6)
         for copy in skip_copies():
             copy.wait_recv()
         take_over()
@@ -570,12 +539,13 @@
 
 def shards(features, section_packs):
     fields = jnp.swapaxes(features[0], 1, 2)
-    packs = jnp.pad(jnp.swapaxes(section_packs[0], 0, 1), ((0, 6), (0, 0)))
+    packs = jnp.pad(jnp.swapaxes(section_packs[0], 0, 1), ((0, 6), (0, LANES - 11520)))
     tables = selections()
     dma = pltpu.SemaphoreType.DMA
     scratch = [
-        pltpu.VMEM((2, 4, 4, 32, 11520), BF16),
+        pltpu.VMEM((2, 4, 4, 32, LANES), BF16),
         pltpu.VMEM((2, 2944, 256), BF16),
+        pltpu.VMEM((5760, 256), BF16),
         pltpu.VMEM((2, 384, 256), BF16),
         pltpu.VMEM((3, 10, 640, 128), BF16),
         pltpu.VMEM((10, 320, 128), BF16),
@@ -593,11 +563,11 @@
         pltpu.VMEM((8, 320, 128), BF16),
         pltpu.VMEM((4, 128, 320), BF16),
         pltpu.VMEM((4, 32, 320), BF16),
-        pltpu.VMEM((6, 8, 8, 128), F32),
-        pltpu.VMEM((6, 8, 8, 128), F32),
-        pltpu.VMEM((8, 128), F32),
-        dma((18, 6)), dma((18, 6)),
-        dma((6, 8)), dma((6, 8)), dma((6, 8)), dma((6, 8)),
+        pltpu.VMEM((6, 64, 2, 128), F32),
+        pltpu.VMEM((2, 128), F32),
+        pltpu.VMEM((2, 128), F32),
+        dma((18, 8)), dma((18, 8)),
+        dma((6,)), dma((6,)), dma((1,)), dma((1,)),
         dma((2,)), dma((2,)), dma((3,)), dma((3,)), dma((3,)), dma((3,)), dma((3,)), dma((1,)),
     ]
     vmem = pl.BlockSpec(memory_space=pltpu.VMEM)

time: 277 us -> 244 us (0.88)
  Pallas kernels: 273 us -> 241 us
    pallas_call x1, Pallas kernels: 273 us -> 241 us  [shards(): pl.pallas_call(kernel, out_shape=jax.ShapeDtypeStruct((4, 32, 320), BF16)...]
where the time goes in v2:
time: 244 us
  Pallas kernels  241 us (99%)
  local copies, waits for them, and re-layouts  3.3 us (1%)
    pallas_call x1, Pallas kernels, shards(): pl.pallas_call(kernel, out_shape=jax.ShapeDtypeStruct((4, 32, 320), BF16)...  241 us

profile of v2, /device:TPU:64, one launch (start us, length us, event | category | flops | bytes accessed | tf_op | source)
XLA Modules:
  0.0 244.1 jit_solution(14036665370496712401)
XLA Ops:
  0.0 1.8 pad.4.w_ref
  1.8 240.8 %shard_map.163 = bf16[4,32,320]{2,1,0:T(8,128)(2,1)} custom-call(bf16[4,320,128]{2,1,0:T(8,128)(2,1)} %bitcast.9, bf16[16,12288]{1,0:T(8,128)(2,1)} %pad.4.w_ref, bf16[320,512]{1,0:T(8,128)(2,1)} %constant.33.clone.sel_di, bf16[320,512]{1,0:T(8,128)(2,1)} %constant.34.clone.sel_nat, bf16[512,320]{1,0:T(8,128)(2,1)} %constant.35.clone.exp_di, ...), custom_call_target="tpu_custom_call" | custom-call | flops 12000000000 | bytes 30000000 | tf_op jit(solution)/shard_map/pallas_call | solution.py:574
  242.6 1.5 copy.19

commit v3 on v2

--- a/solution.py
+++ b/solution.py
@@ -13,19 +13,18 @@
 MESH = pl.DeviceIdType.MESH
 EPSILON = 1e-05
 CHUNK = 1536
-HALF_A = 768
-HALF_B = CHUNK - HALF_A
+HALF = CHUNK // 2
+QUARTER = CHUNK // 4
 ROW_N = 512 * 10
 LANES = 8 * CHUNK
 
 
 def selections():
-    rows = np.arange(512)
-    slot, lane = rows // 16, rows % 16
-    chan_fine = np.where(lane < 10, 10 * ((slot % 16) * 2 + slot // 16) + lane, -1)
-    rows = np.arange(1024)
-    slot, lane = rows // 16, rows % 16
-    chan_wide = np.where(lane < 10, 10 * ((slot % 32) * 2 + slot // 32) + lane, -1)
+    rows = np.arange(768)
+    chan_wide = np.where(rows % 48 < 40, 40 * (rows // 48) + rows % 48, -1)
+    chan_fine = chan_wide[:384]
+    rows = np.arange(48)
+    packed = np.where(rows < 40, 16 * (rows // 10) + rows % 10, -1)
     split = lambda n: np.concatenate([np.arange(0, n, 2), np.arange(1, n, 2)])
     di, di_wide = split(320), split(640)
     nat, nat_wide = np.arange(320), np.arange(640)
@@ -68,6 +67,7 @@
     wide_groups = eq(nat_wide // 20, group)
     bf = lambda m: np.asarray(m, np.float32).astype(jnp.bfloat16)
     return (
+        bf(eq(packed, np.arange(64))),
         bf(eq(di, chan_fine)),
         bf(eq(nat, chan_fine)),
         bf(eq(chan_fine, di)),
@@ -96,9 +96,9 @@
 
 
 def kernel(
-    x_ref, w_ref, sel_di, sel_nat, exp_di, exp_nat, sel_c, exp_c, perm_x, perm_c, shifts, strided,
+    x_ref, w_ref, pack, sel_di, sel_nat, exp_di, exp_nat, sel_c, exp_c, perm_x, perm_c, shifts, strided,
     doubled, taps_one, taps_two, fine_groups, wide_groups, out_ref,
-    W, col, colw, colj, sh, xr, xd, hid, skd, skn, skb, cb, tile, a3, a2, hs, acc, ud, outs, landed,
+    W, raw, col, colw, colj, sh, xr, xd, hid, skd, skn, skb, cb, tile, a3, a2, hs, acc, ud, outs, landed,
     SA, HS, HR, gather_send, gather_recv, a_send, a_recv, b_send, b_recv,
     x_send, x_recv, c_send, c_recv, k_send, k_recv, o_send, o_recv,
 ):
@@ -132,7 +132,7 @@
 
     lax.fori_loop(1, 64, greet, 0)
 
-    W[c, y, x, pl.ds(pl.multiple_of(16 * z, 16), 16), :] = w_ref[...]
+    raw[2 * z + c] = w_ref[...]
     pl.semaphore_wait(barrier, len(peers) + 63)
 
     def remote(src, dst, send, recv, peer):
@@ -219,69 +219,80 @@
 
     chunks = jnp.where(sec == 0, 4, jnp.where(sec == 3, 5, 8))
 
-    def gather_copies(stage, k):
-        lane = lambda off, size: pl.ds(pl.multiple_of(k * CHUNK + off, 128), size)
-        whole, part_a, part_b = lane(0, CHUNK), lane(0, HALF_A), lane(HALF_A, HALF_B)
-        to_xp, to_xm = space(y, xp, z, c), space(y, xm, z, c)
-        to_yp, to_ym = space(yp, x, z, c), space(ym, x, z, c)
-        all32, first, second = pl.ds(0, 32), pl.ds(0, 16), pl.ds(16, 16)
-        every, low, high = pl.ds(0, 4), pl.ds(0, 2), pl.ds(2, 2)
+    def gather_copies(core, stage, k):
+        lanes = lambda off, size: pl.ds(pl.multiple_of(k * CHUNK + off, 128), size)
+        mine, other = lanes(HALF * core, HALF), lanes(HALF * (1 - core), HALF)
+        left, right = lanes(HALF * core, QUARTER), lanes(HALF * core + QUARTER, QUARTER)
+        along_x = (space(y, xp, z, c), space(y, xm, z, c))
+        along_y = (space(yp, x, z, c), space(ym, x, z, c))
+        rows, every = pl.ds(0, 48), pl.ds(0, 4)
+        array = W
         if stage == 0:
-            moves = [((c, y, x, pl.ds(pl.multiple_of(16 * z, 16), 16), whole), space(y, x, 1 - z, c))]
+            array, whole = raw, pl.ds(0, 16)
+            moves = [
+                ((2 * z + c, whole, mine), space(y, x, 1 - z, c)),
+                ((2 * z + c, whole, other), space(y, x, 1 - z, 1 - c)),
+                ((2 * z + c, whole, other), space(y, x, z, 1 - c)),
+            ]
         elif stage == 1:
-            a, b = (c, y, x, all32, part_a), (c, y, x, all32, part_b)
-            moves = [(a, to_xp), (a, to_xm), (b, to_yp), (b, to_ym)]
+            moves = [((y, x, rows, mine), peer) for peer in (along_y if core else along_x)]
+        elif stage == 2 and core == 0:
+            moves = [((y, xm, rows, left), along_x[0]), ((y, xp, rows, right), along_x[1])]
         elif stage == 2:
-            moves = [
-                ((c, y, xm, first, part_a), to_xp),
-                ((c, y, xp, second, part_a), to_xm),
-                ((c, ym, x, first, part_b), to_yp),
-                ((c, yp, x, second, part_b), to_ym),
-            ]
+            moves = [((ym, x, rows, left), along_y[0]), ((yp, x, rows, right), along_y[1])]
+        elif stage == 3 and core == 0:
+            moves = [((y, every, rows, mine), peer) for peer in along_y]
         elif stage == 3:
-            a, b = (c, y, every, all32, part_a), (c, every, x, all32, part_b)
-            moves = [(a, to_yp), (a, to_ym), (b, to_xp), (b, to_xm)]
+            moves = [((every, x, rows, mine), peer) for peer in along_x]
+        elif stage == 4 and core == 0:
+            moves = [((ym, every, rows, left), along_y[0]), ((yp, every, rows, right), along_y[1])]
         elif stage == 4:
-            moves = [
-                ((c, ym, low, all32, part_a), to_yp),
-                ((c, yp, high, all32, part_a), to_ym),
-                ((c, low, xm, all32, part_b), to_xp),
-                ((c, high, xp, all32, part_b), to_xm),
-            ]
+            moves = [((every, xm, rows, left), along_x[0]), ((every, xp, rows, right), along_x[1])]
         else:
-            moves = [((c, every, every, all32, whole), space(y, x, z, 1 - c))]
-        first_id = (0, 1, 5, 9, 13, 17)[stage]
+            moves = [((every, every, rows, mine), space(y, x, z, 1 - c))]
+        first_id = (0, 3, 5, 7, 9, 11)[stage]
         return [
             remote(
-                W.at[where], W.at[where], gather_send.at[first_id + i, k],
+                array.at[where], array.at[where], gather_send.at[first_id + i, k],
                 gather_recv.at[first_id + i, k], (sec, peer),
             )
             for i, (where, peer) in enumerate(moves)
         ]
 
+    def gather_step(core, t):
+        for stage in range(7):
+            k = t - stage
+
+            @pl.when((k >= 0) & (k < chunks))
+            def _():
+                if stage > 0:
+                    for copy in gather_copies(core, stage - 1, k):
+                        copy.wait_recv()
+                if stage == 1:
+                    lanes = pl.ds(pl.multiple_of(k * CHUNK + HALF * core, 128), HALF)
+                    blocks = raw[:, :, lanes].reshape(64, HALF)
+                    W[y, x, :, lanes] = dot(pack[...], blocks).astype(BF16)
+                if stage < 6:
+                    for copy in gather_copies(core, stage, k):
+                        copy.start()
+
     def gather(first, last):
         def step(t, carry):
-            for stage in range(7):
-                k = t - stage
-
-                @pl.when((k >= 0) & (k < chunks))
-                def _():
-                    if stage > 0:
-                        for copy in gather_copies(stage - 1, k):
-                            copy.wait_recv()
-                    if stage < 6:
-                        for copy in gather_copies(stage, k):
-                            copy.start()
-
+            for core in range(2):
+                pl.when(c == core)(lambda core=core: gather_step(core, t))
             return carry
 
         lax.fori_loop(first, last, step, 0)
 
     def gather_end():
+        def waits(core, k):
+            for stage in range(6):
+                for copy in gather_copies(core, stage, k):
+                    copy.wait_send()
+
         def step(k, carry):
-            for stage in range(6):
-                for copy in gather_copies(stage, k):
-                    copy.wait_send()
+            for core in range(2):
+                pl.when(c == core)(lambda core=core: waits(core, k))
             return carry
 
         lax.fori_loop(0, chunks, step, 0)
@@ -319,8 +330,8 @@
     def weighted(lane_start, depth, source):
         total = None
         for p in range(2):
-            kernels = W[:, 2 * p : 2 * p + 2, :, :, lane_start : lane_start + depth]
-            made = dot(kernels.reshape(512, depth), source[p, 0:depth, :])
+            kernels = W[2 * p : 2 * p + 2, :, :, lane_start : lane_start + depth]
+            made = dot(kernels.reshape(384, depth), source[p, 0:depth, :])
             total = made if total is None else total + made
         return total
 
@@ -376,9 +387,9 @@
             hid[2 * q + 1] = packed[:, 128:256]
 
         fine_conv(4, narrow_pieces, 160, 0, 0, 1536, follow, keep_hidden)
+        start_exchange(1, *part_sums([hid[r].astype(F32) for r in range(2, 6)], groups, ROW_N))
         gather(7, 8)
-        sums = part_sums([hid[r].astype(F32) for r in range(2, 6)], groups, ROW_N)
-        mean, rstd = columns(groups, exchanged(1, *sums, ROW_N))
+        mean, rstd = columns(groups, finish_exchange(1, ROW_N))
         activate_rows(hid, 8, -2, mean, rstd)
 
         def keep_skip(q, made):
@@ -399,7 +410,7 @@
                 at = 64 + (dy * 3 + dx) * 320
                 made = dot(skn[dy], strided[0, dx]) + dot(skn[2 + dy], strided[1, dx])
                 col[0, at : at + 320, 0:128] = made.astype(BF16)
-        made = dot(W[:, :, :, :, 2816:5760].reshape(1024, 2944), col[0, :, 0:128])
+        made = dot(W[:, :, :, 2816:5760].reshape(768, 2944), col[0, :, 0:128])
         rounded = (made * narrow_scale).astype(BF16)
         tile[...] = dot(sel_c[...], rounded).astype(BF16)
         hand_over(128 * 20)
@@ -422,7 +433,7 @@
             colw[640 * t : 640 * t + 640, :] = dot(a3[...], taps_one[t]).astype(BF16)
         for i in range(3):
             lanes = slice(1920 * i, 1920 * i + 1920)
-            made = dot(W[:, :, :, :, lanes].reshape(1024, 1920), colw[lanes, :])
+            made = dot(W[:, :, :, lanes].reshape(768, 1920), colw[lanes, :])
             acc[...] = made if i == 0 else acc[...] + made
         rounded = (acc[...] * wide_scale).astype(BF16)
         hs[...] = dot(sel_c[...], rounded)
@@ -437,7 +448,7 @@
         for i in range(3):
             lanes = slice(5760 + 1920 * i, 5760 + 1920 * i + 1920)
             source = colw[1920 * i : 1920 * i + 1920, 0:128]
-            made = dot(W[:, :, :, :, lanes].reshape(1024, 1920), source)
+            made = dot(W[:, :, :, lanes].reshape(768, 1920), source)
             acc[:, 0:128] = made if i == 0 else acc[:, 0:128] + made
         own = dot(exp_c[...], cb[1])
         rounded = (own + acc[:, 0:128] * wide_scale).astype(BF16)
@@ -543,7 +554,8 @@
     tables = selections()
     dma = pltpu.SemaphoreType.DMA
     scratch = [
-        pltpu.VMEM((2, 4, 4, 32, LANES), BF16),
+        pltpu.VMEM((4, 4, 48, LANES), BF16),
+        pltpu.VMEM((4, 16, LANES), BF16),
         pltpu.VMEM((2, 2944, 256), BF16),
         pltpu.VMEM((5760, 256), BF16),
         pltpu.VMEM((2, 384, 256), BF16),
@@ -559,14 +571,14 @@
         pltpu.VMEM((640, 384), BF16),
         pltpu.VMEM((640, 256), BF16),
         pltpu.VMEM((640, 256), F32),
-        pltpu.VMEM((1024, 256), F32),
+        pltpu.VMEM((768, 256), F32),
         pltpu.VMEM((8, 320, 128), BF16),
         pltpu.VMEM((4, 128, 320), BF16),
         pltpu.VMEM((4, 32, 320), BF16),
         pltpu.VMEM((6, 64, 2, 128), F32),
         pltpu.VMEM((2, 128), F32),
         pltpu.VMEM((2, 128), F32),
-        dma((18, 8)), dma((18, 8)),
+        dma((12, 8)), dma((12, 8)),
         dma((6,)), dma((6,)), dma((1,)), dma((1,)),
         dma((2,)), dma((2,)), dma((3,)), dma((3,)), dma((3,)), dma((3,)), dma((3,)), dma((1,)),
     ]

time: 244 us -> 227 us (0.930)
  Pallas kernels: 241 us -> 224 us
    pallas_call x1, Pallas kernels: 241 us -> 224 us  [shards(): pl.pallas_call(kernel, out_shape=jax.ShapeDtypeStruct((4, 32, 320), BF16)...]
where the time goes in v3:
time: 227 us
  Pallas kernels  224 us (99%)
  local copies, waits for them, and re-layouts  3.3 us (1%)
    pallas_call x1, Pallas kernels, shards(): pl.pallas_call(kernel, out_shape=jax.ShapeDtypeStruct((4, 32, 320), BF16)...  224 us

profile of v3, /device:TPU:64, one launch (start us, length us, event | category | flops | bytes accessed | tf_op | source)
XLA Modules:
  0.0 227.1 jit_solution(5774592926249163903)
XLA Ops:
  0.0 1.8 pad.4.w_ref
  1.8 223.8 %shard_map.172 = bf16[4,32,320]{2,1,0:T(8,128)(2,1)} custom-call(bf16[4,320,128]{2,1,0:T(8,128)(2,1)} %bitcast.9, bf16[16,12288]{1,0:T(8,128)(2,1)} %pad.4.w_ref, bf16[48,64]{1,0:T(8,128)(2,1)} %constant.35.clone.pack, bf16[320,384]{1,0:T(8,128)(2,1)} %constant.36.clone.sel_di, bf16[320,384]{1,0:T(8,128)(2,1)} %constant.37.clone.sel_nat, ...), custom_call_target="tpu_custom_call" | custom-call | flops 12000000000 | bytes 30000000 | tf_op jit(solution)/shard_map/pallas_call | solution.py:586
  225.6 1.5 copy.20

commit v4 on v3

--- a/solution.py
+++ b/solution.py
@@ -49,14 +49,14 @@
         ]
     )
 
-    def taps(rows_in, rows_out):
-        a, c = np.arange(rows_in * 64), np.arange(rows_out * 64)
+    def taps():
+        a, c = np.arange(6 * 64), np.arange(2 * 64)
         out = []
         for dy in (0, 1, 2):
             for dx in (-1, 0, 1):
                 col = c % 64 + dx
                 out.append(
-                    eq(a, (c // 64 + dy) * 64 + col) & ((col >= 0) & (col < 64))[None, :]
+                    eq(a, (c // 64 + 1 + dy) * 64 + col) & ((col >= 0) & (col < 64))[None, :]
                 )
         return np.stack(out)
 
@@ -79,8 +79,7 @@
         bf(shifts),
         bf(strided),
         bf(doubled),
-        bf(taps(6, 4)),
-        bf(taps(4, 2)),
+        bf(taps()),
         np.asarray(fine_groups, np.float32),
         np.asarray(wide_groups, np.float32),
     )
@@ -97,10 +96,10 @@
 
 def kernel(
     x_ref, w_ref, pack, sel_di, sel_nat, exp_di, exp_nat, sel_c, exp_c, perm_x, perm_c, shifts, strided,
-    doubled, taps_one, taps_two, fine_groups, wide_groups, out_ref,
-    W, raw, col, colw, colj, sh, xr, xd, hid, skd, skn, skb, cb, tile, a3, a2, hs, acc, ud, outs, landed,
+    doubled, taps, fine_groups, wide_groups, out_ref,
+    W, raw, col, colw, colj, sh, xr, xd, hid, skd, skn, skb, cb, ht, tile, a3, ud, outs, landed,
     SA, HS, HR, gather_send, gather_recv, a_send, a_recv, b_send, b_recv,
-    x_send, x_recv, c_send, c_recv, k_send, k_recv, o_send, o_recv,
+    x_send, x_recv, h_send, h_recv, c_send, c_recv, k_send, k_recv, o_send, o_recv,
 ):
     sec = lax.axis_index("section")
     d = lax.axis_index("space")
@@ -188,6 +187,25 @@
     def across_copy():
         return remote(HS, HR, b_send.at[0], b_recv.at[0], (after, d))
 
+    def rim_copies(kind, array, down, up):
+        (down_from, down_to), (up_from, up_to) = down, up
+        return [
+            remote(array.at[pl.ds(down_from, size)], array.at[pl.ds(down_to, size)],
+                   h_send.at[kind, 0], h_recv.at[kind, 0], (sec, below))
+            for size in (2 if kind == 0 else 1,)
+        ] + [
+            remote(array.at[pl.ds(up_from, 1)], array.at[pl.ds(up_to, 1)],
+                   h_send.at[kind, 1], h_recv.at[kind, 1], (sec, above))
+        ]
+
+    def start_all(copies):
+        for copy in copies:
+            copy.start()
+
+    def wait_all(copies):
+        for copy in copies:
+            copy.wait()
+
     def tile_copies():
         return [
             remote(tile, cb.at[slot], c_send.at[slot], c_recv.at[slot], (after, peer))
@@ -197,8 +215,8 @@
     def skip_copies():
         return [
             remote(skd.at[lax_rows(1, 4)], skb.at[lax_rows(2, 4)], k_send.at[0], k_recv.at[0], (before, d)),
-            remote(skd.at[lax_rows(3, 2)], skb.at[lax_rows(0, 2)], k_send.at[1], k_recv.at[1], (before, below)),
-            remote(skd.at[lax_rows(1, 2)], skb.at[lax_rows(6, 2)], k_send.at[2], k_recv.at[2], (before, above)),
+            remote(skd.at[lax_rows(4, 1)], skb.at[lax_rows(1, 1)], k_send.at[1], k_recv.at[1], (before, below)),
+            remote(skd.at[lax_rows(1, 1)], skb.at[lax_rows(6, 1)], k_send.at[2], k_recv.at[2], (before, above)),
         ]
 
     def lax_rows(start, size):
@@ -207,14 +225,19 @@
     def hand_over(count):
         for copy in tile_copies():
             copy.start()
-        mean, deviation = part_sums([tile[...].astype(F32)], wide_groups[...], count)
-        HS[...] = jnp.concatenate(exchanged(2, mean, deviation, count), axis=0)
-        across_copy().start()
-        for copy in tile_copies() + [across_copy()]:
+
+        @pl.when(sec < 2)
+        def _():
+            mean, deviation = part_sums([tile[...].astype(F32)], wide_groups[...], count)
+            HS[...] = jnp.concatenate(exchanged(2, mean, deviation, count), axis=0)
+            across_copy().start()
+            across_copy().wait_send()
+
+        for copy in tile_copies():
             copy.wait_send()
 
     def take_over():
-        for copy in tile_copies() + [across_copy()]:
+        for copy in tile_copies():
             copy.wait_recv()
 
     chunks = jnp.where(sec == 0, 4, jnp.where(sec == 3, 5, 8))
@@ -345,25 +368,25 @@
     def row_kept(row):
         return jnp.where(row < 0, keep_top, jnp.where(row > 3, keep_bottom, 1.0))
 
-    def activate_rows(source, count, first_row, mean, rstd):
+    def activate_rows(source, start, stop, own_row, mean, rstd):
         def one(r, carry):
-            values = activate(source[r].astype(F32), mean, rstd) * row_kept(r + first_row)
+            values = activate(source[r].astype(F32), mean, rstd) * row_kept(r - own_row)
             put_shifted(r, 0, values.astype(BF16))
             return carry
 
-        lax.fori_loop(0, count, one, 0)
+        lax.fori_loop(start, stop, one, 0)
 
     @pl.when(sec == 0)
     def _():
         x_copies = [
-            remote(x_ref.at[pl.ds(1, 3)], xr.at[pl.ds(0, 3)], x_send.at[0], x_recv.at[0], (0, below)),
-            remote(x_ref.at[pl.ds(0, 2)], xr.at[pl.ds(7, 2)], x_send.at[1], x_recv.at[1], (0, above)),
+            remote(x_ref.at[pl.ds(3, 1)], xr.at[pl.ds(2, 1)], x_send.at[0], x_recv.at[0], (0, below)),
+            remote(x_ref.at[pl.ds(0, 1)], xr.at[pl.ds(7, 1)], x_send.at[1], x_recv.at[1], (0, above)),
         ]
         for copy in x_copies:
             copy.start()
         for r in range(4):
             xr[3 + r] = x_ref[r]
-        xr[9] = jnp.zeros((320, 128), BF16)
+        hid[7] = jnp.zeros((320, 128), BF16)
 
         def permute(r, carry):
             xd[r] = dot(perm_x[...], xr[r]).astype(BF16)
@@ -375,22 +398,26 @@
         gather(0, 7)
         for copy in x_copies:
             copy.wait()
-        lax.fori_loop(0, 3, permute, 0)
-        lax.fori_loop(7, 10, permute, 0)
+        lax.fori_loop(2, 3, permute, 0)
+        lax.fori_loop(7, 8, permute, 0)
         mean, rstd = columns(groups, finish_exchange(0, ROW_N))
-        activate_rows(xd, 10, -3, mean, rstd)
+        activate_rows(xd, 2, 8, 3, mean, rstd)
 
         def keep_hidden(q, made):
             rounded = (made * narrow_scale).astype(BF16)
             packed = dot(sel_di[...], rounded).astype(BF16)
-            hid[2 * q] = packed[:, 0:128]
-            hid[2 * q + 1] = packed[:, 128:256]
-
-        fine_conv(4, narrow_pieces, 160, 0, 0, 1536, follow, keep_hidden)
+            hid[2 * q + 2] = packed[:, 0:128]
+            hid[2 * q + 3] = packed[:, 128:256]
+
+        from_two = lambda q, off: 2 * q + off + 2
+        fine_conv(2, narrow_pieces, 160, 0, 0, 1536, from_two, keep_hidden)
+        rims = rim_copies(0, hid, (4, 0), (2, 6))
+        start_all(rims)
         start_exchange(1, *part_sums([hid[r].astype(F32) for r in range(2, 6)], groups, ROW_N))
         gather(7, 8)
         mean, rstd = columns(groups, finish_exchange(1, ROW_N))
-        activate_rows(hid, 8, -2, mean, rstd)
+        wait_all(rims)
+        activate_rows(hid, 0, 8, 2, mean, rstd)
 
         def keep_skip(q, made):
             for j in range(2):
@@ -400,8 +427,6 @@
                 skn[2 * q + j] = dot(sel_nat[...], rounded).astype(BF16)
 
         fine_conv(3, narrow_pieces, 160, 32, 1408, 1536, follow, keep_skip)
-        for copy in skip_copies():
-            copy.start()
         gather(8, 10)
         skn[0] = (skn[0].astype(F32) * keep_top).astype(BF16)
         col[0, 0:64, 0:128] = jnp.zeros((64, 128), BF16)
@@ -414,6 +439,7 @@
         rounded = (made * narrow_scale).astype(BF16)
         tile[...] = dot(sel_c[...], rounded).astype(BF16)
         hand_over(128 * 20)
+        start_all(skip_copies())
         for copy in skip_copies():
             copy.wait_send()
 
@@ -423,35 +449,41 @@
         take_over()
         count = 128 * 20
         groups = wide_groups[...]
+        across_copy().wait_recv()
         mean, rstd = columns(groups, [HR[0:1, :], HR[1:2, :]])
-        for i in range(3):
-            values = activate(cb[i].astype(F32), mean, rstd)
-            values = values * (keep_top, 1.0, keep_bottom)[i]
-            a3[:, 128 * i : 128 * i + 128] = values.astype(BF16)
-
-        for t in range(9):
-            colw[640 * t : 640 * t + 640, :] = dot(a3[...], taps_one[t]).astype(BF16)
-        for i in range(3):
-            lanes = slice(1920 * i, 1920 * i + 1920)
-            made = dot(W[:, :, :, lanes].reshape(768, 1920), colw[lanes, :])
-            acc[...] = made if i == 0 else acc[...] + made
-        rounded = (acc[...] * wide_scale).astype(BF16)
-        hs[...] = dot(sel_c[...], rounded)
-        column = lax.broadcasted_iota(jnp.int32, (1, 256), 1)
-        inner = jnp.where((column >= 64) & (column < 192), 1.0, 0.0)
-        kept = jnp.where(column < 64, keep_top, jnp.where(column >= 192, keep_bottom, 1.0))
-        sums = part_sums([hs[...]], groups, count, inner)
+
+        def activate_tiles(source):
+            for i in range(3):
+                values = activate(source[i].astype(F32), mean, rstd)
+                values = values * (keep_top, 1.0, keep_bottom)[i]
+                a3[:, 128 * i : 128 * i + 128] = values.astype(BF16)
+
+        def coarse_conv(lane_start):
+            for t in range(9):
+                px = ((0, 256), (128, 256), (128, 384))[t // 3]
+                moved = dot(a3[:, px[0] : px[1]], taps[t, px[0] : px[1], :])
+                colw[640 * t : 640 * t + 640, :] = moved.astype(BF16)
+            total = None
+            for i in range(3):
+                lanes = slice(lane_start + 1920 * i, lane_start + 1920 * i + 1920)
+                source = colw[1920 * i : 1920 * i + 1920, :]
+                made = dot(W[:, :, :, lanes].reshape(768, 1920), source)
+                total = made if total is None else total + made
+            return total * wide_scale
+
+        activate_tiles(cb)
+        rounded = coarse_conv(0).astype(BF16)
+        hidden = dot(sel_c[...], rounded)
+        ht[1] = hidden.astype(BF16)
+        rims = rim_copies(3, ht, (1, 0), (1, 2))
+        start_all(rims)
+        sums = part_sums([hidden], groups, count)
         mean, rstd = columns(groups, exchanged(3, *sums, count))
-        a2[...] = (activate(hs[...], mean, rstd) * kept).astype(BF16)
-        for t in range(9):
-            colw[640 * t : 640 * t + 640, 0:128] = dot(a2[...], taps_two[t]).astype(BF16)
-        for i in range(3):
-            lanes = slice(5760 + 1920 * i, 5760 + 1920 * i + 1920)
-            source = colw[1920 * i : 1920 * i + 1920, 0:128]
-            made = dot(W[:, :, :, lanes].reshape(768, 1920), source)
-            acc[:, 0:128] = made if i == 0 else acc[:, 0:128] + made
+        wait_all(rims)
+        activate_tiles(ht)
+        made = coarse_conv(5760)
         own = dot(exp_c[...], cb[1])
-        rounded = (own + acc[:, 0:128] * wide_scale).astype(BF16)
+        rounded = (own + made).astype(BF16)
         tile[...] = dot(sel_c[...], rounded).astype(BF16)
         hand_over(count)
 
@@ -472,22 +504,25 @@
         for i in range(3):
             moved = dot(perm_c[...], cb[i]) * (keep_top, 1.0, keep_bottom)[i]
             moved = moved.astype(BF16)
-            for half in range(2):
+            for half in ((1,), (0, 1), (0,))[i]:
                 for dx in range(3):
                     sh[dx, 2 * i + half] = dot(moved, doubled[half, dx]).astype(BF16)
 
         def keep_upper(q, made):
             rounded = (made * wide_scale).astype(BF16)
             packed = dot(sel_di[...], rounded).astype(BF16)
-            ud[2 * q] = packed[:, 0:128]
-            ud[2 * q + 1] = packed[:, 128:256]
-
-        half_row = lambda q, off: q + (off + 1) // 2
-        fine_conv(4, wide_pieces, 320, 0, 0, 2944, half_row, keep_upper)
+            ud[2 * q + 2] = packed[:, 0:128]
+            ud[2 * q + 3] = packed[:, 128:256]
+
+        half_row = lambda q, off: q + 1 + (off + 1) // 2
+        fine_conv(2, wide_pieces, 320, 0, 0, 2944, half_row, keep_upper)
+        rims = rim_copies(1, ud, (5, 1), (2, 6))
+        start_all(rims)
         groups_u, groups_s = fine_groups[1], fine_groups[2]
         mean_u, dev_u = part_sums([ud[r].astype(F32) for r in range(2, 6)], groups_u, 2 * ROW_N)
         mean_s, dev_s = part_sums([skb[r].astype(F32) for r in range(2, 6)], groups_s, 2 * ROW_N)
         rows = exchanged(4, mean_u + mean_s, dev_u + dev_s, 2 * ROW_N)
+        wait_all(rims)
         mean_u, rstd_u = columns(groups_u, rows)
         mean_s, rstd_s = columns(groups_s, rows)
 
@@ -499,19 +534,23 @@
             put_shifted(r, 320, lower.astype(BF16))
             return carry
 
-        lax.fori_loop(0, 8, joined_row, 0)
+        lax.fori_loop(1, 7, joined_row, 0)
 
         def keep_hidden(q, made):
             rounded = (made * wide_scale).astype(BF16)
             packed = dot(sel_di[...], rounded).astype(BF16)
-            hid[2 * q] = packed[:, 0:128]
-            hid[2 * q + 1] = packed[:, 128:256]
-
-        fine_conv(3, joined_pieces, 320, 64, 2816, 2944, follow, keep_hidden)
+            hid[2 * q + 1] = packed[:, 0:128]
+            hid[2 * q + 2] = packed[:, 128:256]
+
+        from_one = lambda q, off: 2 * q + off + 1
+        fine_conv(2, joined_pieces, 320, 64, 2816, 2944, from_one, keep_hidden)
+        rims = rim_copies(2, hid, (4, 0), (1, 5))
+        start_all(rims)
         groups = fine_groups[0]
         sums = part_sums([hid[r].astype(F32) for r in range(1, 5)], groups, ROW_N)
         mean, rstd = columns(groups, exchanged(5, *sums, ROW_N))
-        activate_rows(hid, 6, -1, mean, rstd)
+        wait_all(rims)
+        activate_rows(hid, 0, 6, 1, mean, rstd)
         for p in range(2):
             colj[p, 0:32, :] = jnp.zeros((32, 256), BF16)
             colj[p, 352:384, :] = jnp.zeros((32, 256), BF16)
@@ -557,7 +596,7 @@
         pltpu.VMEM((4, 4, 48, LANES), BF16),
         pltpu.VMEM((4, 16, LANES), BF16),
         pltpu.VMEM((2, 2944, 256), BF16),
-        pltpu.VMEM((5760, 256), BF16),
+        pltpu.VMEM((5760, 128), BF16),
         pltpu.VMEM((2, 384, 256), BF16),
         pltpu.VMEM((3, 10, 640, 128), BF16),
         pltpu.VMEM((10, 320, 128), BF16),
@@ -567,11 +606,9 @@
         pltpu.VMEM((6, 320, 128), BF16),
         pltpu.VMEM((8, 320, 128), BF16),
         pltpu.VMEM((3, 640, 128), BF16),
+        pltpu.VMEM((3, 640, 128), BF16),
         pltpu.VMEM((640, 128), BF16),
         pltpu.VMEM((640, 384), BF16),
-        pltpu.VMEM((640, 256), BF16),
-        pltpu.VMEM((640, 256), F32),
-        pltpu.VMEM((768, 256), F32),
         pltpu.VMEM((8, 320, 128), BF16),
         pltpu.VMEM((4, 128, 320), BF16),
         pltpu.VMEM((4, 32, 320), BF16),
@@ -580,7 +617,7 @@
         pltpu.VMEM((2, 128), F32),
         dma((12, 8)), dma((12, 8)),
         dma((6,)), dma((6,)), dma((1,)), dma((1,)),
-        dma((2,)), dma((2,)), dma((3,)), dma((3,)), dma((3,)), dma((3,)), dma((3,)), dma((1,)),
+        dma((2,)), dma((2,)), dma((4, 2)), dma((4, 2)), dma((3,)), dma((3,)), dma((3,)), dma((3,)), dma((3,)), dma((1,)),
     ]
     vmem = pl.BlockSpec(memory_space=pltpu.VMEM)
     out = pl.pallas_call(

time: 227 us -> 199 us (0.88)
  Pallas kernels: 224 us -> 196 us
    pallas_call x1, Pallas kernels: 224 us -> 196 us  [shards(): pl.pallas_call(kernel, out_shape=jax.ShapeDtypeStruct((4, 32, 320), BF16)...]
where the time goes in v4:
time: 199 us
  Pallas kernels  196 us (98%)
  local copies, waits for them, and re-layouts  3.3 us (2%)
    pallas_call x1, Pallas kernels, shards(): pl.pallas_call(kernel, out_shape=jax.ShapeDtypeStruct((4, 32, 320), BF16)...  196 us

profile of v4, /device:TPU:64, one launch (start us, length us, event | category | flops | bytes accessed | tf_op | source)
XLA Modules:
  0.0 198.9 jit_solution(14845431916163855823)
XLA Ops:
  0.0 1.8 pad.4.w_ref
  1.8 195.6 %shard_map.163 = bf16[4,32,320]{2,1,0:T(8,128)(2,1)} custom-call(bf16[4,320,128]{2,1,0:T(8,128)(2,1)} %bitcast.9, bf16[16,12288]{1,0:T(8,128)(2,1)} %pad.4.w_ref, bf16[48,64]{1,0:T(8,128)(2,1)} %constant.33.clone.pack, bf16[320,384]{1,0:T(8,128)(2,1)} %constant.34.clone.sel_di, bf16[320,384]{1,0:T(8,128)(2,1)} %constant.35.clone.sel_nat, ...), custom_call_target="tpu_custom_call" | custom-call | flops 12000000000 | bytes 30000000 | tf_op jit(solution)/shard_map/pallas_call | solution.py:623
  197.4 1.5 copy.19

commit v5 on v4

--- a/solution.py
+++ b/solution.py
@@ -98,7 +98,7 @@
     x_ref, w_ref, pack, sel_di, sel_nat, exp_di, exp_nat, sel_c, exp_c, perm_x, perm_c, shifts, strided,
     doubled, taps, fine_groups, wide_groups, out_ref,
     W, raw, col, colw, colj, sh, xr, xd, hid, skd, skn, skb, cb, ht, tile, a3, ud, outs, landed,
-    SA, HS, HR, gather_send, gather_recv, a_send, a_recv, b_send, b_recv,
+    SA, SB, HS, gather_send, gather_recv, a_send, a_recv, b_send, b_recv,
     x_send, x_recv, h_send, h_recv, c_send, c_recv, k_send, k_recv, o_send, o_recv,
 ):
     sec = lax.axis_index("section")
@@ -111,6 +111,9 @@
     xp, xm = lax.rem(x + 1, 4), lax.rem(x + 3, 4)
     yp, ym = lax.rem(y + 1, 4), lax.rem(y + 3, 4)
     below, above = lax.rem(d + 1, 64), lax.rem(d + 63, 64)
+    hi, lo = lax.div(d, 8), lax.rem(d, 8)
+    lo_peer = lambda k: hi * 8 + lax.rem(lo + k, 8)
+    hi_peer = lambda k: lax.rem(hi + k, 8) * 8 + lo
     after, before = lax.rem(sec + 1, 4), lax.rem(sec + 3, 4)
     is_top = d == 0
     is_bottom = d == 63
@@ -118,21 +121,17 @@
     keep_bottom = jnp.where(is_bottom, 0.0, 1.0)
 
     barrier = pltpu.get_barrier_semaphore()
-    peers = [(lax.rem(sec + 2, 4), d)]
+    peers = [(sec, lo_peer(k)) for k in range(1, 8)] + [(sec, hi_peer(k)) for k in range(1, 8)]
+    peers += [(sec, space(y, xp, z, c)), (sec, space(y, xm, z, c)), (sec, below), (sec, above)]
     for other in (after, before):
-        peers += [(other, d), (other, below), (other, above)]
+        peers += [(other, hi_peer(k)) for k in range(8)] + [(other, below), (other, above)]
+    peers += [(lax.rem(sec + 2, 4), d)]
     for peer in peers:
         pl.semaphore_signal(barrier, inc=1, device_id=peer, device_id_type=MESH)
 
-    def greet(k, carry):
-        peer = (sec, lax.rem(d + k, 64))
-        pl.semaphore_signal(barrier, inc=1, device_id=peer, device_id_type=MESH)
-        return carry
-
-    lax.fori_loop(1, 64, greet, 0)
-
-    raw[2 * z + c] = w_ref[...]
-    pl.semaphore_wait(barrier, len(peers) + 63)
+    raw[2 * z + c] = jnp.zeros((16, LANES), BF16)
+    raw[2 * z + c, 0:10, 0:11520] = w_ref[...]
+    pl.semaphore_wait(barrier, len(peers))
 
     def remote(src, dst, send, recv, peer):
         return pltpu.make_async_remote_copy(
@@ -142,10 +141,9 @@
 
     def combined(messages, count):
         means = messages[:, 0:1, :]
-        mean = jnp.sum(means, axis=0) * (1.0 / 64)
+        mean = jnp.sum(means, axis=0) * 0.125
         spread = jnp.sum(jnp.square(means - mean[None]), axis=0) * count
-        squares = jnp.sum(messages[:, 1:2, :], axis=0) + spread
-        return mean, lax.rsqrt(squares * (1.0 / (64 * count)) + EPSILON)
+        return jnp.concatenate([mean, jnp.sum(messages[:, 1:2, :], axis=0) + spread], axis=0)
 
     def part_sums(blocks, groups, count, weight=None):
         total = blocks[0] if weight is None else blocks[0] * weight
@@ -162,30 +160,51 @@
         channel = jnp.sum(squares, axis=1, keepdims=True)
         return mean, jnp.sum(groups * channel, axis=0, keepdims=True)
 
-    def start_exchange(e, mean, deviation):
+    def first_copies(e):
+        return [
+            remote(SA.at[e, 0], SA.at[e, k], a_send.at[e, k], a_recv.at[e, k], (sec, lo_peer(k)))
+            for k in range(1, 8)
+        ]
+
+    def second_copies(e):
+        return [
+            remote(SB.at[e, 0], SB.at[e, k], b_send.at[e, k], b_recv.at[e, k], (sec, hi_peer(k)))
+            for k in range(1, 8)
+        ]
+
+    def start_first(e, mean, deviation):
         SA[e, 0] = jnp.concatenate([mean, deviation], axis=0)
-
-        def one(k, carry):
-            peer = (sec, lax.rem(d + k, 64))
-            remote(SA.at[e, 0], SA.at[e, k], a_send.at[e], a_recv.at[e], peer).start()
-            return carry
-
-        lax.fori_loop(1, 64, one, 0)
-
-    def finish_exchange(e, count):
-        others = SA.at[e, pl.ds(1, 63)]
-        remote(others, others, a_send.at[e], a_recv.at[e], (sec, below)).wait()
+        start_all(first_copies(e))
+
+    def finish_first(e, count):
+        wait_all(first_copies(e))
         return combined(SA[e], count)
 
+    def start_second(e, count):
+        SB[e, 0] = finish_first(e, count)
+        start_all(second_copies(e))
+
+    def scale_rows(e, count):
+        total = combined(SB[e], 8 * count)
+        return total[0:1, :], lax.rsqrt(total[1:2, :] * (1.0 / (64 * count)) + EPSILON)
+
+    def finish_second(e, count):
+        wait_all(second_copies(e))
+        return scale_rows(e, count)
+
     def exchanged(e, mean, deviation, count):
-        start_exchange(e, mean, deviation)
-        return finish_exchange(e, count)
+        start_first(e, mean, deviation)
+        start_second(e, count)
+        return finish_second(e, count)
 
     def columns(groups, rows):
         return [jnp.sum(groups * row, axis=1, keepdims=True) for row in rows]
 
-    def across_copy():
-        return remote(HS, HR, b_send.at[0], b_recv.at[0], (after, d))
+    def across_copies():
+        return [
+            remote(HS, SB.at[2, k], b_send.at[2, k], b_recv.at[2, k], (after, hi_peer(k)))
+            for k in range(8)
+        ]
 
     def rim_copies(kind, array, down, up):
         (down_from, down_to), (up_from, up_to) = down, up
@@ -229,9 +248,11 @@
         @pl.when(sec < 2)
         def _():
             mean, deviation = part_sums([tile[...].astype(F32)], wide_groups[...], count)
-            HS[...] = jnp.concatenate(exchanged(2, mean, deviation, count), axis=0)
-            across_copy().start()
-            across_copy().wait_send()
+            start_first(2, mean, deviation)
+            HS[...] = finish_first(2, count)
+            start_all(across_copies())
+            for copy in across_copies():
+                copy.wait_send()
 
         for copy in tile_copies():
             copy.wait_send()
@@ -249,7 +270,11 @@
         along_x = (space(y, xp, z, c), space(y, xm, z, c))
         along_y = (space(yp, x, z, c), space(ym, x, z, c))
         rows, every = pl.ds(0, 48), pl.ds(0, 4)
-        array = W
+        array, sibling = W, space(y, x, z, 1 - c)
+
+        def line(core, at, lanes=mine):
+            return (every, at, rows, lanes) if core else (at, every, rows, lanes)
+
         if stage == 0:
             array, whole = raw, pl.ds(0, 16)
             moves = [
@@ -263,17 +288,17 @@
             moves = [((y, xm, rows, left), along_x[0]), ((y, xp, rows, right), along_x[1])]
         elif stage == 2:
             moves = [((ym, x, rows, left), along_y[0]), ((yp, x, rows, right), along_y[1])]
-        elif stage == 3 and core == 0:
-            moves = [((y, every, rows, mine), peer) for peer in along_y]
         elif stage == 3:
-            moves = [((every, x, rows, mine), peer) for peer in along_x]
-        elif stage == 4 and core == 0:
-            moves = [((ym, every, rows, left), along_y[0]), ((yp, every, rows, right), along_y[1])]
+            own = line(core, x if core else y)
+            moves = [(own, peer) for peer in (along_x if core else along_y)] + [(own, sibling)]
         elif stage == 4:
-            moves = [((every, xm, rows, left), along_x[0]), ((every, xp, rows, right), along_x[1])]
+            up, down = (xm, xp) if core else (ym, yp)
+            to_next, to_last = along_x if core else along_y
+            moves = [(line(core, up, left), to_next), (line(core, down, right), to_last)]
+            moves += [(line(core, up), sibling), (line(core, down), sibling)]
         else:
-            moves = [((every, every, rows, mine), space(y, x, z, 1 - c))]
-        first_id = (0, 3, 5, 7, 9, 11)[stage]
+            moves = [(line(core, lax.rem((x if core else y) + 2, 4)), sibling)]
+        first_id = (0, 3, 5, 7, 10, 14)[stage]
         return [
             remote(
                 array.at[where], array.at[where], gather_send.at[first_id + i, k],
@@ -284,9 +309,10 @@
 
     def gather_step(core, t):
         for stage in range(7):
-            k = t - stage
-
-            @pl.when((k >= 0) & (k < chunks))
+            turn = t - stage
+            k = jnp.maximum(turn - 2, 0)
+
+            @pl.when((turn == 0) | ((turn > 2) & (k < chunks)))
             def _():
                 if stage > 0:
                     for copy in gather_copies(core, stage - 1, k):
@@ -382,6 +408,7 @@
             remote(x_ref.at[pl.ds(3, 1)], xr.at[pl.ds(2, 1)], x_send.at[0], x_recv.at[0], (0, below)),
             remote(x_ref.at[pl.ds(0, 1)], xr.at[pl.ds(7, 1)], x_send.at[1], x_recv.at[1], (0, above)),
         ]
+        gather(0, 1)
         for copy in x_copies:
             copy.start()
         for r in range(4):
@@ -394,13 +421,15 @@
 
         lax.fori_loop(3, 7, permute, 0)
         groups = fine_groups[0]
-        start_exchange(0, *part_sums([xd[r].astype(F32) for r in range(3, 7)], groups, ROW_N))
-        gather(0, 7)
+        start_first(0, *part_sums([xd[r].astype(F32) for r in range(3, 7)], groups, ROW_N))
+        gather(1, 4)
+        start_second(0, ROW_N)
+        gather(4, 7)
         for copy in x_copies:
             copy.wait()
         lax.fori_loop(2, 3, permute, 0)
         lax.fori_loop(7, 8, permute, 0)
-        mean, rstd = columns(groups, finish_exchange(0, ROW_N))
+        mean, rstd = columns(groups, finish_second(0, ROW_N))
         activate_rows(xd, 2, 8, 3, mean, rstd)
 
         def keep_hidden(q, made):
@@ -413,9 +442,11 @@
         fine_conv(2, narrow_pieces, 160, 0, 0, 1536, from_two, keep_hidden)
         rims = rim_copies(0, hid, (4, 0), (2, 6))
         start_all(rims)
-        start_exchange(1, *part_sums([hid[r].astype(F32) for r in range(2, 6)], groups, ROW_N))
+        start_first(1, *part_sums([hid[r].astype(F32) for r in range(2, 6)], groups, ROW_N))
         gather(7, 8)
-        mean, rstd = columns(groups, finish_exchange(1, ROW_N))
+        start_second(1, ROW_N)
+        gather(8, 10)
+        mean, rstd = columns(groups, finish_second(1, ROW_N))
         wait_all(rims)
         activate_rows(hid, 0, 8, 2, mean, rstd)
 
@@ -427,7 +458,7 @@
                 skn[2 * q + j] = dot(sel_nat[...], rounded).astype(BF16)
 
         fine_conv(3, narrow_pieces, 160, 32, 1408, 1536, follow, keep_skip)
-        gather(8, 10)
+        gather(10, 12)
         skn[0] = (skn[0].astype(F32) * keep_top).astype(BF16)
         col[0, 0:64, 0:128] = jnp.zeros((64, 128), BF16)
         for dy in range(3):
@@ -445,12 +476,13 @@
 
     @pl.when((sec == 1) | (sec == 2))
     def _():
-        gather(0, chunks + 6)
+        gather(0, jnp.where(sec == 1, 14, chunks + 8))
         take_over()
         count = 128 * 20
         groups = wide_groups[...]
-        across_copy().wait_recv()
-        mean, rstd = columns(groups, [HR[0:1, :], HR[1:2, :]])
+        for copy in across_copies():
+            copy.wait_recv()
+        mean, rstd = columns(groups, scale_rows(2, count))
 
         def activate_tiles(source):
             for i in range(3):
@@ -478,7 +510,14 @@
         rims = rim_copies(3, ht, (1, 0), (1, 2))
         start_all(rims)
         sums = part_sums([hidden], groups, count)
-        mean, rstd = columns(groups, exchanged(3, *sums, count))
+        start_first(3, *sums)
+        start_second(3, count)
+
+        @pl.when(sec == 1)
+        def _():
+            gather(14, 16)
+
+        mean, rstd = columns(groups, finish_second(3, count))
         wait_all(rims)
         activate_tiles(ht)
         made = coarse_conv(5760)
@@ -497,7 +536,7 @@
 
     @pl.when(sec == 3)
     def _():
-        gather(0, chunks + 6)
+        gather(0, chunks + 8)
         for copy in skip_copies():
             copy.wait_recv()
         take_over()
@@ -589,7 +628,7 @@
 
 def shards(features, section_packs):
     fields = jnp.swapaxes(features[0], 1, 2)
-    packs = jnp.pad(jnp.swapaxes(section_packs[0], 0, 1), ((0, 6), (0, LANES - 11520)))
+    packs = jnp.swapaxes(section_packs[0], 0, 1)
     tables = selections()
     dma = pltpu.SemaphoreType.DMA
     scratch = [
@@ -612,11 +651,11 @@
         pltpu.VMEM((8, 320, 128), BF16),
         pltpu.VMEM((4, 128, 320), BF16),
         pltpu.VMEM((4, 32, 320), BF16),
-        pltpu.VMEM((6, 64, 2, 128), F32),
+        pltpu.VMEM((6, 8, 2, 128), F32),
+        pltpu.VMEM((6, 8, 2, 128), F32),
         pltpu.VMEM((2, 128), F32),
-        pltpu.VMEM((2, 128), F32),
-        dma((12, 8)), dma((12, 8)),
-        dma((6,)), dma((6,)), dma((1,)), dma((1,)),
+        dma((15, 8)), dma((15, 8)),
+        dma((6, 8)), dma((6, 8)), dma((6, 8)), dma((6, 8)),
         dma((2,)), dma((2,)), dma((4, 2)), dma((4, 2)), dma((3,)), dma((3,)), dma((3,)), dma((3,)), dma((3,)), dma((1,)),
     ]
     vmem = pl.BlockSpec(memory_space=pltpu.VMEM)

time: 199 us -> 201 us (1.010)
  Pallas kernels: 196 us -> 199 us
    pallas_call x1, Pallas kernels: 196 us -> 199 us  [shards(): pl.pallas_call(kernel, out_shape=jax.ShapeDtypeStruct((4, 32, 320), BF16)...]
where the time goes in v5:
time: 201 us; the launch traced here: 200 us
  Pallas kernels  199 us (99%)
    pallas_call x1, Pallas kernels, shards(): pl.pallas_call(kernel, out_shape=jax.ShapeDtypeStruct((4, 32, 320), BF16)...  199 us

profile of v5, /device:TPU:64, one launch (start us, length us, event | category | flops | bytes accessed | tf_op | source)
XLA Modules:
  0.0 200.4 jit_solution(2361329729199374786)
XLA Ops:
  0.0 198.8 %shard_map.163 = bf16[4,32,320]{2,1,0:T(8,128)(2,1)} custom-call(bf16[4,320,128]{2,1,0:T(8,128)(2,1)} %bitcast.9, bf16[10,11520]{1,0:T(8,128)(2,1)} %bitcast.8, bf16[48,64]{1,0:T(8,128)(2,1)} %constant.30.clone.pack, bf16[320,384]{1,0:T(8,128)(2,1)} %constant.31.clone.sel_di, bf16[320,384]{1,0:T(8,128)(2,1)} %constant.32.clone.sel_nat, ...), custom_call_target="tpu_custom_call" | custom-call | flops 12000000000 | bytes 30000000 | tf_op jit(solution)/shard_map/pallas_call | solution.py:662
  198.8 1.5 copy.19

commit v6 on v4

--- a/solution.py
+++ b/solution.py
@@ -1,3 +1,4 @@
+import functools
 import math
 
 import jax
@@ -95,7 +96,7 @@
 
 
 def kernel(
-    x_ref, w_ref, pack, sel_di, sel_nat, exp_di, exp_nat, sel_c, exp_c, perm_x, perm_c, shifts, strided,
+    loads,     x_ref, w_ref, pack, sel_di, sel_nat, exp_di, exp_nat, sel_c, exp_c, perm_x, perm_c, shifts, strided,
     doubled, taps, fine_groups, wide_groups, out_ref,
     W, raw, col, colw, colj, sh, xr, xd, hid, skd, skn, skb, cb, ht, tile, a3, ud, outs, landed,
     SA, HS, HR, gather_send, gather_recv, a_send, a_recv, b_send, b_recv,
@@ -117,6 +118,9 @@
     keep_top = jnp.where(is_top, 0.0, 1.0)
     keep_bottom = jnp.where(is_bottom, 0.0, 1.0)
 
+    for load in loads:
+        load.start()
+
     barrier = pltpu.get_barrier_semaphore()
     peers = [(lax.rem(sec + 2, 4), d)]
     for other in (after, before):
@@ -131,7 +135,10 @@
 
     lax.fori_loop(1, 64, greet, 0)
 
-    raw[2 * z + c] = w_ref[...]
+    raw[2 * z + c] = jnp.zeros((16, LANES), BF16)
+    raw[2 * z + c, 0:10, 0:11520] = w_ref[...]
+    for load in loads:
+        load.wait()
     pl.semaphore_wait(barrier, len(peers) + 63)
 
     def remote(src, dst, send, recv, peer):
@@ -587,12 +594,24 @@
     gather_end()
 
 
+def entry(count, x_ref, w_ref, *refs):
+    sources, out_ref, copies = refs[:count], refs[count], refs[count + 1 : 2 * count + 1]
+    sems, others = refs[2 * count + 1], refs[2 * count + 2 :]
+    loads = [
+        pltpu.make_async_copy(source, copy, sems.at[i])
+        for i, (source, copy) in enumerate(zip(sources, copies))
+    ]
+    kernel(loads, x_ref, w_ref, *copies, out_ref, *others)
+
+
 def shards(features, section_packs):
     fields = jnp.swapaxes(features[0], 1, 2)
-    packs = jnp.pad(jnp.swapaxes(section_packs[0], 0, 1), ((0, 6), (0, LANES - 11520)))
+    packs = jnp.swapaxes(section_packs[0], 0, 1)
     tables = selections()
     dma = pltpu.SemaphoreType.DMA
-    scratch = [
+    scratch = [pltpu.VMEM(table.shape, table.dtype) for table in tables]
+    scratch += [
+        dma((len(tables),)),
         pltpu.VMEM((4, 4, 48, LANES), BF16),
         pltpu.VMEM((4, 16, LANES), BF16),
         pltpu.VMEM((2, 2944, 256), BF16),
@@ -621,9 +640,9 @@
     ]
     vmem = pl.BlockSpec(memory_space=pltpu.VMEM)
     out = pl.pallas_call(
-        kernel,
+        functools.partial(entry, len(tables)),
         out_shape=jax.ShapeDtypeStruct((4, 32, 320), BF16),
-        in_specs=[vmem] * (2 + len(tables)),
+        in_specs=[vmem] * 2 + [pl.BlockSpec(memory_space=pl.ANY)] * len(tables),
         out_specs=vmem,
         scratch_shapes=scratch,
         compiler_params=pltpu.CompilerParams(

time: 199 us -> 196 us (0.985)
  no operation moved by 1% of the time
where the time goes in v6:
time: 196 us
  Pallas kernels  195 us (99%)
    pallas_call x1, Pallas kernels, shards(): pl.pallas_call(functools.partial(entry, len(tables)), out_shape=jax.Shape...  195 us

profile of v6, /device:TPU:64, one launch (start us, length us, event | category | flops | bytes accessed | tf_op | source)
XLA Modules:
  0.0 196.1 jit_solution(5540867301781727703)
XLA Ops:
  0.0 194.5 %shard_map.163 = bf16[4,32,320]{2,1,0:T(8,128)(2,1)} custom-call(bf16[4,320,128]{2,1,0:T(8,128)(2,1)} %bitcast.9, bf16[10,11520]{1,0:T(8,128)(2,1)} %bitcast.8, bf16[48,64]{1,0:T(8,128)(2,1)} %constant.30.clone.refs_0_, bf16[320,384]{1,0:T(8,128)(2,1)} %constant.31.clone.refs_1_, bf16[320,384]{1,0:T(8,128)(2,1)} %constant.32.clone.refs_2_, ...), custom_call_target="tpu_custom_call" | custom-call | flops 12000000000 | bytes 30000000 | tf_op jit(solution)/shard_map/pallas_call | solution.py:642
  194.5 1.5 copy.19

commit v7 on v6

--- a/solution.py
+++ b/solution.py
@@ -391,6 +391,7 @@
         ]
         for copy in x_copies:
             copy.start()
+        gather(0, 1)
         for r in range(4):
             xr[3 + r] = x_ref[r]
         hid[7] = jnp.zeros((320, 128), BF16)
@@ -401,8 +402,10 @@
 
         lax.fori_loop(3, 7, permute, 0)
         groups = fine_groups[0]
-        start_exchange(0, *part_sums([xd[r].astype(F32) for r in range(3, 7)], groups, ROW_N))
-        gather(0, 7)
+        sums = part_sums([xd[r].astype(F32) for r in range(3, 7)], groups, ROW_N)
+        gather(1, 2)
+        start_exchange(0, *sums)
+        gather(2, 7)
         for copy in x_copies:
             copy.wait()
         lax.fori_loop(2, 3, permute, 0)

time: 196 us -> 196 us (level)
  no operation moved by 1% of the time
where the time goes in v7:
time: 196 us
  Pallas kernels  194 us (99%)
    pallas_call x1, Pallas kernels, shards(): pl.pallas_call(functools.partial(entry, len(tables)), out_shape=jax.Shape...  194 us

profile of v7, /device:TPU:64, one launch (start us, length us, event | category | flops | bytes accessed | tf_op | source)
XLA Modules:
  0.0 195.7 jit_solution(14452389438111545520)
XLA Ops:
  0.0 194.1 %shard_map.163 = bf16[4,32,320]{2,1,0:T(8,128)(2,1)} custom-call(bf16[4,320,128]{2,1,0:T(8,128)(2,1)} %bitcast.9, bf16[10,11520]{1,0:T(8,128)(2,1)} %bitcast.8, bf16[48,64]{1,0:T(8,128)(2,1)} %constant.30.clone.refs_0_, bf16[320,384]{1,0:T(8,128)(2,1)} %constant.31.clone.refs_1_, bf16[320,384]{1,0:T(8,128)(2,1)} %constant.32.clone.refs_2_, ...), custom_call_target="tpu_custom_call" | custom-call | flops 12000000000 | bytes 30000000 | tf_op jit(solution)/shard_map/pallas_call | solution.py:645
  194.2 1.5 copy.19

commit v8 on v7

--- a/solution.py
+++ b/solution.py
@@ -256,7 +256,11 @@
         along_x = (space(y, xp, z, c), space(y, xm, z, c))
         along_y = (space(yp, x, z, c), space(ym, x, z, c))
         rows, every = pl.ds(0, 48), pl.ds(0, 4)
-        array = W
+        array, sibling = W, space(y, x, z, 1 - c)
+
+        def line(core, at, lanes=mine):
+            return (every, at, rows, lanes) if core else (at, every, rows, lanes)
+
         if stage == 0:
             array, whole = raw, pl.ds(0, 16)
             moves = [
@@ -270,17 +274,17 @@
             moves = [((y, xm, rows, left), along_x[0]), ((y, xp, rows, right), along_x[1])]
         elif stage == 2:
             moves = [((ym, x, rows, left), along_y[0]), ((yp, x, rows, right), along_y[1])]
-        elif stage == 3 and core == 0:
-            moves = [((y, every, rows, mine), peer) for peer in along_y]
         elif stage == 3:
-            moves = [((every, x, rows, mine), peer) for peer in along_x]
-        elif stage == 4 and core == 0:
-            moves = [((ym, every, rows, left), along_y[0]), ((yp, every, rows, right), along_y[1])]
+            own = line(core, x if core else y)
+            moves = [(own, peer) for peer in (along_x if core else along_y)] + [(own, sibling)]
         elif stage == 4:
-            moves = [((every, xm, rows, left), along_x[0]), ((every, xp, rows, right), along_x[1])]
+            up, down = (xm, xp) if core else (ym, yp)
+            to_next, to_last = along_x if core else along_y
+            moves = [(line(core, up, left), to_next), (line(core, down, right), to_last)]
+            moves += [(line(core, up), sibling), (line(core, down), sibling)]
         else:
-            moves = [((every, every, rows, mine), space(y, x, z, 1 - c))]
-        first_id = (0, 3, 5, 7, 9, 11)[stage]
+            moves = [(line(core, lax.rem((x if core else y) + 2, 4)), sibling)]
+        first_id = (0, 3, 5, 7, 10, 14)[stage]
         return [
             remote(
                 array.at[where], array.at[where], gather_send.at[first_id + i, k],
@@ -637,7 +641,7 @@
         pltpu.VMEM((6, 64, 2, 128), F32),
         pltpu.VMEM((2, 128), F32),
         pltpu.VMEM((2, 128), F32),
-        dma((12, 8)), dma((12, 8)),
+        dma((15, 8)), dma((15, 8)),
         dma((6,)), dma((6,)), dma((1,)), dma((1,)),
         dma((2,)), dma((2,)), dma((4, 2)), dma((4, 2)), dma((3,)), dma((3,)), dma((3,)), dma((3,)), dma((3,)), dma((1,)),
     ]

time: 196 us -> 195 us (level)
  no operation moved by 1% of the time
where the time goes in v8:
time: 195 us
  Pallas kernels  193 us (99%)
    pallas_call x1, Pallas kernels, shards(): pl.pallas_call(functools.partial(entry, len(tables)), out_shape=jax.Shape...  193 us

profile of v8, /device:TPU:64, one launch (start us, length us, event | category | flops | bytes accessed | tf_op | source)
XLA Modules:
  0.0 194.9 jit_solution(7722770755691591438)
XLA Ops:
  0.0 193.4 %shard_map.163 = bf16[4,32,320]{2,1,0:T(8,128)(2,1)} custom-call(bf16[4,320,128]{2,1,0:T(8,128)(2,1)} %bitcast.9, bf16[10,11520]{1,0:T(8,128)(2,1)} %bitcast.8, bf16[48,64]{1,0:T(8,128)(2,1)} %constant.30.clone.refs_0_, bf16[320,384]{1,0:T(8,128)(2,1)} %constant.31.clone.refs_1_, bf16[320,384]{1,0:T(8,128)(2,1)} %constant.32.clone.refs_2_, ...), custom_call_target="tpu_custom_call" | custom-call | flops 12000000000 | bytes 30000000 | tf_op jit(solution)/shard_map/pallas_call | solution.py:649
  193.4 1.5 copy.19

commit v9 on v8

--- a/solution.py
+++ b/solution.py
@@ -492,11 +492,12 @@
         rims = rim_copies(3, ht, (1, 0), (1, 2))
         start_all(rims)
         sums = part_sums([hidden], groups, count)
-        mean, rstd = columns(groups, exchanged(3, *sums, count))
+        start_exchange(3, *sums)
+        own = dot(exp_c[...], cb[1])
+        mean, rstd = columns(groups, finish_exchange(3, count))
         wait_all(rims)
         activate_tiles(ht)
         made = coarse_conv(5760)
-        own = dot(exp_c[...], cb[1])
         rounded = (own + made).astype(BF16)
         tile[...] = dot(sel_c[...], rounded).astype(BF16)
         hand_over(count)
@@ -514,6 +515,8 @@
         gather(0, chunks + 6)
         for copy in skip_copies():
             copy.wait_recv()
+        groups_u, groups_s = fine_groups[1], fine_groups[2]
+        mean_s, dev_s = part_sums([skb[r].astype(F32) for r in range(2, 6)], groups_s, 2 * ROW_N)
         take_over()
         for i in range(3):
             moved = dot(perm_c[...], cb[i]) * (keep_top, 1.0, keep_bottom)[i]
@@ -532,9 +535,7 @@
         fine_conv(2, wide_pieces, 320, 0, 0, 2944, half_row, keep_upper)
         rims = rim_copies(1, ud, (5, 1), (2, 6))
         start_all(rims)
-        groups_u, groups_s = fine_groups[1], fine_groups[2]
         mean_u, dev_u = part_sums([ud[r].astype(F32) for r in range(2, 6)], groups_u, 2 * ROW_N)
-        mean_s, dev_s = part_sums([skb[r].astype(F32) for r in range(2, 6)], groups_s, 2 * ROW_N)
         rows = exchanged(4, mean_u + mean_s, dev_u + dev_s, 2 * ROW_N)
         wait_all(rims)
         mean_u, rstd_u = columns(groups_u, rows)

time: 195 us -> 195 us (level)
  no operation moved by 1% of the time
where the time goes in v9:
time: 195 us
  Pallas kernels  193 us (99%)
    pallas_call x1, Pallas kernels, shards(): pl.pallas_call(functools.partial(entry, len(tables)), out_shape=jax.Shape...  193 us

profile of v9, /device:TPU:64, one launch (start us, length us, event | category | flops | bytes accessed | tf_op | source)
XLA Modules:
  0.0 194.9 jit_solution(4285566737640173651)
XLA Ops:
  0.0 193.3 %shard_map.163 = bf16[4,32,320]{2,1,0:T(8,128)(2,1)} custom-call(bf16[4,320,128]{2,1,0:T(8,128)(2,1)} %bitcast.9, bf16[10,11520]{1,0:T(8,128)(2,1)} %bitcast.8, bf16[48,64]{1,0:T(8,128)(2,1)} %constant.30.clone.refs_0_, bf16[320,384]{1,0:T(8,128)(2,1)} %constant.31.clone.refs_1_, bf16[320,384]{1,0:T(8,128)(2,1)} %constant.32.clone.refs_2_, ...), custom_call_target="tpu_custom_call" | custom-call | flops 12000000000 | bytes 30000000 | tf_op jit(solution)/shard_map/pallas_call | solution.py:650
  193.3 1.5 copy.19
